TPU v7x, 32 devices: a whole 2x2x4 slice. The times are simulated.
32 devices in a mesh: grp: 4 (over y, x), dev: 8 (over z, core).
Axes of the slice: x: 2, y: 2, z: 4, core: 2. Of those that a mesh axis runs over, the one named last changes fastest.
Arguments:
- queries: bfloat16 [4096, 4096], P('dev', 'grp'), may hold values from -120 to 120
- keys: bfloat16 [4096, 512], P('dev', 'grp'), may hold values from -4.5 to 4.5
- values: bfloat16 [4096, 512], P('dev', 'grp'), may hold values from -6 to 6
- doc_ids: int32 [4096], replicated, may hold values from 0 to 15, never falling along the last dimension, each value on 1 to 2560 neighbouring positions
- out_weight: bfloat16 [4096, 2048], P('grp'), may hold values from -0.5 to 0.5
- norm_gain: float32 [2048], replicated, may hold values from 0.1 to 1.9
- expert_ids: int32 [8, 512, 8], P('dev', 'grp'), may hold values from 0 to 31, all different within a row; in each aligned block of 128 rows (0 to 127, 128 to 255, ..., all dimensions but the last counted through in order) at most 48 rows name the same one
- gate_values: float32 [8, 512, 8], P('dev', 'grp'), may hold values from 0.05 to 0.5
- expert_gate: bfloat16 [32, 2048, 768], P(('grp', 'dev')), may hold values from -0.125 to 0.125
- expert_up: bfloat16 [32, 2048, 768], P(('grp', 'dev')), may hold values from -0.125 to 0.125
- expert_down: bfloat16 [32, 768, 2048], P(('grp', 'dev')), may hold values from -0.21875 to 0.21875
Outputs:
- final: bfloat16 [8, 512, 2048], P('dev', 'grp')
Inputs may be any that keep to these rules, and one draw needn't show every extreme that they name: doc_ids never fall along the tokens; every document has 1 to 2560 tokens and one has exactly 2560. `expert_ids`: each token names 8 different experts; among the 128 tokens of one device no expert is named by more than 48 tokens, and some expert reaches 48.
All inputs are finite; a program needn't handle non-finite values.
Results may differ from a plain program's by a relative error of at most 0.017.
Values may be sent and summed in bfloat16 or wider, within the bound.
No kernel may reach another device: no remote copies, remote signals or barrier semaphores. Data moves between devices by JAX's collectives and lax.ppermute only.
A program may use at most 128 MiB of HBM per device.

v0:
```python
import functools
import math

import jax
import jax.numpy as jnp
from jax import lax
from jax.experimental import pallas as pl
from jax.experimental.pallas import tpu as pltpu
from jax.sharding import PartitionSpec as P

HEAD_SIZE = 128
KEY_BLOCK = 512
SPLIT = 8
IN_TILE = 256
OUT_TILE = 512
VMEM_BYTES = 56 * 1024 * 1024
LOW = -1e30


def after(value, *others):
    return lax.optimization_barrier((value, *others))[0]


def swap_x(value):
    return lax.ppermute(value, "grp", [(i, i ^ 1) for i in range(lax.axis_size("grp"))])


def swap_y(value):
    return lax.ppermute(value, "grp", [(i, i ^ 2) for i in range(lax.axis_size("grp"))])


def swap_core(value):
    return lax.ppermute(value, "dev", [(i, i ^ 1) for i in range(lax.axis_size("dev"))])


def turn(value, planes):
    count = lax.axis_size("dev")
    return lax.ppermute(value, "dev", [(i, (i - 2 * planes) % count) for i in range(count)])


def earlier(value, steps, sources=lambda source: True):
    count = lax.axis_size("dev")
    pairs = [(i, i + steps) for i in range(count - steps) if sources(i)]
    return lax.ppermute(value, "dev", pairs)


def hold_kernel(*refs):
    del refs


def hold(values, *waits):
    anywhere = pl.BlockSpec(memory_space=pl.ANY)
    return pl.pallas_call(
        hold_kernel,
        in_specs=[anywhere] * (len(values) + len(waits)),
        out_specs=[anywhere] * len(values),
        out_shape=[jax.ShapeDtypeStruct(v.shape, v.dtype) for v in values],
        input_output_aliases={i: i for i in range(len(values))},
        cost_estimate=pl.CostEstimate(flops=0, bytes_accessed=0, transcendentals=0),
        name="hold",
    )(*values, *waits)


def gather_keys(keys, values, reach):
    own = jnp.concatenate([keys, values], axis=1)
    whole = reach // 2
    lanes = [own]
    for _ in range(whole):
        lanes.append(earlier(lanes[-1], 2))
    pieces = [piece for lane in lanes[::-1] for piece in (lane, swap_core(lane))]
    if reach % 2:
        pieces = [earlier(own, reach, lambda source: source % 2 == 1)] + pieces
    return pieces


def attend_kernel(bounds, *refs, shards, waits, mask):
    q_ref, start_ref = refs[:2]
    pieces = refs[2 : 2 + shards]
    out_ref, q_all, kv_ref, top, total = refs[2 + shards + waits :]
    size = pieces[0].shape[0]
    core = bounds[2]
    for i, piece in enumerate(pieces):
        lone = shards % 2
        if i < lone:
            at = 0
        else:
            pair = i - (i - lone) % 2
            at = pair + (core if pair == i else 1 - core)
        kv_ref[pl.ds(pl.multiple_of(at * size, size), size), :] = piece[...]
    rows = q_ref.shape[0]
    heads = q_ref.shape[1] // HEAD_SIZE
    for h in range(heads):
        q_all[h * rows : (h + 1) * rows, :] = q_ref[:, h * HEAD_SIZE : (h + 1) * HEAD_SIZE]
    top[...] = jnp.full_like(top, LOW)
    total[...] = jnp.zeros_like(total)
    block_index = bounds[1] ^ mask
    q_low = bounds[0] + block_index * rows
    first_start, last_start = bounds[3 + 2 * block_index], bounds[4 + 2 * block_index]
    factor = math.log2(math.e) / math.sqrt(HEAD_SIZE)

    def step(block, masked):
        low = pl.multiple_of(block * KEY_BLOCK, KEY_BLOCK)
        key = kv_ref[pl.ds(low, KEY_BLOCK), :HEAD_SIZE]
        value = kv_ref[pl.ds(low, KEY_BLOCK), HEAD_SIZE:]
        value = jnp.concatenate([value, jnp.ones_like(value)], axis=1)
        if masked:
            key_pos = low + lax.broadcasted_iota(jnp.int32, (rows, KEY_BLOCK), 1)
            q_pos = q_low + lax.broadcasted_iota(jnp.int32, (rows, KEY_BLOCK), 0)
            seen = (key_pos >= start_ref[...]) & (key_pos <= q_pos)
        part_heads = heads // SPLIT
        size = part_heads * rows
        scores = []
        for r in range(SPLIT):
            scores.append(lax.dot_general(
                q_all[r * size : (r + 1) * size, :], key, (((1,), (1,)), ((), ())), preferred_element_type=jnp.float32
            ))
        for r in range(SPLIT):
            span = slice(r * size, (r + 1) * size)
            score = scores[r] * factor
            if masked:
                score = jnp.where(seen[None], score.reshape(part_heads, rows, KEY_BLOCK), LOW)
                score = score.reshape(size, KEY_BLOCK)
            old = top[span, :]
            new = jnp.maximum(old, jnp.max(score, axis=1, keepdims=True))
            weight = jnp.exp2(score - jnp.concatenate([new] * (KEY_BLOCK // HEAD_SIZE), axis=1))
            shrink = jnp.exp2(old - new)
            added = jnp.dot(weight.astype(jnp.bfloat16), value, preferred_element_type=jnp.float32)
            total[span, :] = total[span, :] * jnp.concatenate([shrink, shrink], axis=1) + added
            top[span, :] = new

    def loop(low, high, masked):
        def body(block, carry):
            step(block, masked)
            return carry

        lax.fori_loop(low, high, body, 0)

    begin = first_start // KEY_BLOCK
    end = (q_low + rows - 1) // KEY_BLOCK + 1
    inner_low = jnp.minimum((last_start + KEY_BLOCK - 1) // KEY_BLOCK, end)
    inner_high = jnp.maximum((q_low + 1) // KEY_BLOCK, inner_low)
    loop(begin, inner_low, True)
    loop(inner_low, inner_high, False)
    loop(inner_high, end, True)
    for h in range(heads):
        part = total[h * rows : (h + 1) * rows, :]
        out_ref[:, h * HEAD_SIZE : (h + 1) * HEAD_SIZE] = (
            part[:, :HEAD_SIZE] / part[:, HEAD_SIZE:]
        ).astype(out_ref.dtype)


def attend(mask, queries, pieces, starts, bounds, rows, waits=()):
    width = queries.shape[1]
    heads = width // HEAD_SIZE
    length = len(pieces) * pieces[0].shape[0]
    pairs = heads * rows * length // 2
    return pl.pallas_call(
        functools.partial(attend_kernel, shards=len(pieces), waits=len(waits), mask=mask),
        grid_spec=pltpu.PrefetchScalarGridSpec(
            num_scalar_prefetch=1,
            grid=(1,),
            in_specs=[
                pl.BlockSpec((rows, width), lambda i, bounds: (bounds[1] ^ mask, 0)),
                pl.BlockSpec((rows, 1), lambda i, bounds: (bounds[1] ^ mask, 0)),
            ]
            + [pl.BlockSpec(p.shape, lambda i, bounds: (0, 0)) for p in pieces]
            + [pl.BlockSpec(memory_space=pl.ANY)] * len(waits),
            out_specs=pl.BlockSpec((rows, width), lambda i, bounds: (0, 0)),
            scratch_shapes=[
                pltpu.VMEM((heads * rows, HEAD_SIZE), jnp.bfloat16),
                pltpu.VMEM((length, 2 * HEAD_SIZE), jnp.bfloat16),
                pltpu.VMEM((heads * rows, HEAD_SIZE), jnp.float32),
                pltpu.VMEM((heads * rows, 2 * HEAD_SIZE), jnp.float32),
            ],
        ),
        out_shape=jax.ShapeDtypeStruct((rows, width), jnp.bfloat16),
        compiler_params=pltpu.CompilerParams(vmem_limit_bytes=VMEM_BYTES),
        cost_estimate=pl.CostEstimate(
            flops=4 * pairs * HEAD_SIZE, bytes_accessed=4 * length * HEAD_SIZE, transcendentals=pairs
        ),
        name="attend",
    )(bounds, queries, starts[:, None], *pieces, *waits)


def feed_kernel(*refs, blocks, first, waits):
    refs = list(refs)
    gates_kept, hidden, gate_buf, up_buf, down_buf, sems = refs[-6:]
    del refs[-6:]
    incoming = [refs.pop(0) for _ in range(5 * blocks)] if first else None
    slot_of, gates, gate_ref, up_ref, down_ref = (refs.pop(0) for _ in range(5))
    if not first:
        taken, earlier_given = refs.pop(0), refs.pop(0)
    refs = refs[waits:]
    if first:
        given, other, taken = refs
    else:
        outgoing, given = refs[: 5 * blocks], refs[5 * blocks]
    loads = [
        pltpu.make_async_copy(source, target, sems.at[i])
        for i, (source, target) in enumerate(
            ((gate_ref, gate_buf), (up_ref, up_buf), (down_ref, down_buf))
        )
    ]
    for load in loads:
        load.start()
    tokens = slot_of.shape[3]
    half = tokens // 2
    slots = given.shape[0] // (2 * blocks)
    each = slots // 2

    def chosen(p, e, b):
        at = 2 * p + b
        mine = slot_of[at // 4, e, at % 4 : at % 4 + 1, :]
        return lax.broadcasted_iota(jnp.int32, (each, tokens), 0) == mine

    def pick(p):
        lines = []
        for e in range(2):
            for b in range(2):
                found = chosen(p, e, b).astype(jnp.float32)
                zeros = jnp.zeros_like(found)
                lines.append(jnp.concatenate([zeros, found] if b else [found, zeros], axis=1))
        return jnp.concatenate(lines).astype(jnp.bfloat16)

    def share(e):
        parts = []
        for p in range(2 * blocks):
            for b in range(2):
                at = 2 * p + b
                gate = gates[at // 4, e, at % 4 : at % 4 + 1, :]
                parts.append(jnp.sum(jnp.where(chosen(p, e, b), gate, 0.0), axis=1, keepdims=True))
        return jnp.concatenate(parts)

    if first:
        for p in range(2 * blocks):
            at = 5 * (p // 2) + 2 * (p % 2)
            held = jnp.concatenate([piece[...] for piece in incoming[at : at + 2 + p % 2]])
            found = jnp.dot(pick(p), held, preferred_element_type=jnp.float32).astype(taken.dtype)
            taken[p * slots : (p + 1) * slots, :] = found[:slots]
            other[p * slots : (p + 1) * slots, :] = found[slots:]

    ff, width = down_buf.shape
    inner, outer = math.gcd(ff, IN_TILE), math.gcd(width, OUT_TILE)

    def tiles(count, body):
        lax.fori_loop(0, count, lambda i, carry: (body(i), carry)[1], 0)

    def gate_tile(i):
        at = pl.ds(pl.multiple_of(i * inner, inner), inner)
        gate = jnp.dot(taken[...], gate_buf[:, at], preferred_element_type=jnp.float32)
        gates_kept[:, at] = gate / (1.0 + jnp.exp(-gate))

    def up_tile(i):
        at = pl.ds(pl.multiple_of(i * inner, inner), inner)
        up = jnp.dot(taken[...], up_buf[:, at], preferred_element_type=jnp.float32)
        hidden[:, at] = (gates_kept[:, at] * up).astype(jnp.bfloat16)

    def down_tile(i):
        at = pl.ds(pl.multiple_of(i * outer, outer), outer)
        part = jnp.dot(hidden[...], down_buf[:, at], preferred_element_type=jnp.float32)
        given[:, at] = (part * shares).astype(given.dtype)

    loads[0].wait()
    tiles(ff // inner, gate_tile)
    loads[1].wait()
    tiles(ff // inner, up_tile)
    shares = share(0 if first else 1)
    loads[2].wait()
    tiles(width // outer, down_tile)
    if not first:
        for p in range(2 * blocks):
            at = 5 * (p // 2) + 2 * (p % 2)
            place = slice(p * slots, (p + 1) * slots)
            rows = jnp.concatenate([earlier_given[place, :], given[place, :]])
            back = lax.dot_general(
                pick(p), rows, (((0,), (0,)), ((), ())), preferred_element_type=jnp.float32
            ).astype(jnp.bfloat16)
            outgoing[at][...] = back[:tokens]
            if p % 2 == 0:
                outgoing[at + 1][...] = back[tokens:]
            else:
                outgoing[at + 1][...] = back[tokens : tokens + half]
                outgoing[at + 2][...] = back[tokens + half :]


def feed(first, inputs, slot_of, gates, slots, weights, extra, rows, waits=()):
    width, ff = weights[0].shape
    blocks = slot_of.shape[0]
    slots = 4 * blocks * slots

    def whole(shape):
        return pl.BlockSpec(shape, lambda i: (0,) * len(shape))

    shapes = ([(rows, width)] * 3 + [(rows // 2, width), (rows - rows // 2, width)]) * blocks
    operands = [*inputs, slot_of, gates, *weights, *extra]
    specs = [whole(v.shape) for v in operands]
    at = len(inputs) + 2
    specs[at : at + 3] = [pl.BlockSpec(memory_space=pl.ANY)] * 3
    specs += [pl.BlockSpec(memory_space=pl.ANY)] * len(waits)
    results = [(slots, width)] * 2 if first else shapes
    kept = pltpu.VMEM((slots, width), jnp.bfloat16)
    return pl.pallas_call(
        functools.partial(feed_kernel, blocks=blocks, first=first, waits=len(waits)),
        grid=(1,),
        in_specs=specs,
        out_specs=[whole(s) for s in results],
        out_shape=[jax.ShapeDtypeStruct(s, jnp.bfloat16) for s in results],
        scratch_shapes=[
            kept,
            pltpu.VMEM((slots, ff), jnp.float32),
            pltpu.VMEM((slots, ff), jnp.bfloat16),
        ]
        + [pltpu.VMEM(w.shape, w.dtype) for w in weights]
        + [pltpu.SemaphoreType.DMA((3,))],
        compiler_params=pltpu.CompilerParams(vmem_limit_bytes=VMEM_BYTES),
        cost_estimate=pl.CostEstimate(
            flops=6 * slots * width * ff,
            bytes_accessed=6 * width * ff + 12 * blocks * rows * width,
            transcendentals=slots * ff,
        ),
        name="feed_first" if first else "feed_second",
    )(*operands, *waits)


def collect_near(own, by_x, by_y, from_a, from_b, *waits):
    half = from_a.shape[0]
    if waits:
        by_x, by_y = hold([by_x, by_y], *waits)
    by_y = jnp.concatenate([by_y[:half] + from_a, by_y[half:]])
    by_x = jnp.concatenate([by_x[:half], by_x[half:] + from_b])
    return own, swap_x(by_x), swap_y(by_y)


def add_up(parts):
    return sum(part.astype(jnp.float32) for part in parts)


def routing(ids, gates, expert_count, waits):
    dev_size = lax.axis_size("dev")
    planes = dev_size // 2
    named = ids.T[None] == jnp.arange(expert_count, dtype=jnp.int32)[:, None, None]
    [dense] = hold([jnp.sum(jnp.where(named, gates.T[None], 0.0), axis=1)], *waits)
    pair = jnp.stack([dense, swap_x(dense)])
    four = jnp.concatenate([pair, swap_y(pair)])
    every = jnp.stack([four] + [turn(four, k) for k in range(1, planes)])
    me = lax.axis_index("grp") * dev_size + lax.axis_index("dev")
    mine = jnp.stack(
        [lax.dynamic_index_in_dim(every, e, 2, keepdims=False) for e in (me, me ^ 1)], axis=1
    )
    named = mine > 0
    tokens = mine.shape[-1]
    before = jnp.triu(jnp.ones((tokens, tokens), jnp.bfloat16), 1)
    rank = jnp.dot(named.astype(jnp.bfloat16), before, preferred_element_type=jnp.float32)
    return jnp.where(named, rank, -1.0).astype(jnp.int32), mine, (pair, four)


def shards(
    queries,
    keys,
    values,
    doc_ids,
    out_weight,
    norm_gain,
    expert_ids,
    gate_values,
    expert_gate,
    expert_up,
    expert_down,
):
    own_rows = queries.shape[0]
    grp_size = lax.axis_size("grp")
    dev_size = lax.axis_size("dev")
    planes = dev_size // 2
    group, device = lax.axis_index("grp"), lax.axis_index("dev")
    dev_rows = own_rows // grp_size
    width = out_weight.shape[1]
    top_count = expert_ids.shape[2]
    expert_count = grp_size * dev_size
    capacity = max(2, 3 * dev_rows * top_count // (2 * expert_count))
    slots = -(-capacity // 16) * 16
    doc_reach = dev_size * own_rows // 2 + own_rows
    reach = min(dev_size - 1, (doc_reach + own_rows - 1) // own_rows)

    pieces = gather_keys(keys, values, reach)
    own_low = (len(pieces) - 2 + device % 2) * own_rows
    own_docs = lax.dynamic_slice_in_dim(doc_ids, device * own_rows, own_rows, 0)
    starts = jnp.sum((doc_ids[None, :] < own_docs[:, None]).astype(jnp.int32), axis=1)
    starts = starts - device * own_rows + own_low
    ends = jnp.stack([starts[::dev_rows], starts[dev_rows - 1 :: dev_rows]], axis=1)
    bounds = jnp.concatenate([jnp.stack([own_low, group, device % 2]), ends.reshape(-1)]).astype(jnp.int32)

    slot_of, gates, steps = routing(expert_ids[0], gate_values[0], expert_count, pieces[-2:])
    own_weights = [expert_gate[0], expert_up[0], expert_down[0]]
    other_weights = [swap_core(w) for w in own_weights]

    def part(mask, *waits):
        attended = attend(mask, queries, pieces, starts, bounds, dev_rows, waits)
        return jnp.dot(attended, out_weight, preferred_element_type=jnp.float32)

    half = dev_rows // 2
    far = part(3).astype(jnp.bfloat16)
    from_a, from_b = swap_x(far[:half]), swap_y(far[half:])
    by_x = part(1, far, steps[0]).astype(jnp.bfloat16)
    by_y = part(2, by_x, steps[1], *other_weights).astype(jnp.bfloat16)
    own = part(0, slot_of, gates, from_a, from_b)
    projected = add_up(collect_near(own, by_x, by_y, from_a, from_b))
    normed = (
        projected
        * lax.rsqrt(jnp.mean(projected * projected, axis=-1, keepdims=True) + 1e-06)
        * norm_gain
    ).astype(jnp.bfloat16)

    order = list(range(planes))
    turned = order[1:] + order[:1]
    sets = [turned[i : i + 2] for i in range(0, planes, 2)]
    blocks, done = {}, {}

    def feed_first(members, *waits):
        routes = [jnp.stack([part[k] for k in members]) for part in (slot_of, gates)]
        inputs = [b for k in members for b in blocks[k]]
        results = feed(True, inputs, *routes, slots, own_weights, [], dev_rows, waits)
        return members, routes, *results

    def feed_second(state, *waits):
        members, routes, given, other = state
        out = feed(False, [], *routes, slots, other_weights, [other, given], dev_rows, waits)
        for i, k in enumerate(members):
            done[k] = out[5 * i : 5 * i + 5]
        return out[0]

    def relay(near, *waits):
        first, second = halves(*near, *waits) if waits else (near[0][:half], near[1][half:])
        return swap_y(first), swap_x(second)

    near, sent, fars = (), [], [(), ()]

    def launch(k):
        nonlocal near
        block = normed
        if k:
            block = jnp.copy(normed)
            if len(sent) > 1:
                [block] = hold([block], *sent[-2])
            [block] = hold([turn(block, k)], *near, *fars[-2])
        near = swap_x(block), swap_y(block)
        blocks[k] = [block]

    def relay(k, *waits):
        nonlocal near
        near = hold(near, *waits) if waits else near
        sent.append((near[0][:half], near[1][half:]))
        far = swap_y(sent[-1][0]), swap_x(sent[-1][1])
        fars.append(far)
        blocks[k] += [*near, *far]
        return far

    launch(0)
    far = relay(0)
    for i, members in enumerate(sets[:-1]):
        for k in members:
            if k not in blocks:
                launch(k)
                relay(k)
        following = next(k for k in sets[i + 1] if k)
        state = feed_first(members)
        launch(following)
        far = relay(following, state[2])
        feed_second(state, *near)

    early = [k for members in sets[:-1][::-1] for k in members[::-1]]
    late = [k for k in sets[-1] if k] + [0]
    froms, sums = {}, []

    def far_part(k):
        froms[k] = swap_x(done[k][3]), swap_y(done[k][4])
        return froms[k]

    def near_part(k, *waits):
        parts = collect_near(*done[k][:3], *froms[k], *waits)
        summed = add_up(parts)
        if k:
            summed = turn(summed.astype(jnp.bfloat16), planes - k).astype(jnp.float32)
        sums.append(summed)
        return parts[1:]

    def held(k, *waits):
        done[k] = [*done[k][:3], *hold(done[k][3:5], *waits)]

    chain = far
    for k in early[:1]:
        held(k, *chain)
        chain = far_part(k)
    state = feed_first(sets[-1], *chain)
    arrived = ()
    for k in early[:1]:
        arrived = near_part(k)
    for k in early[1:]:
        held(k, *chain)
        chain = far_part(k)
    feed_second(state, *arrived, *chain)
    for k in early[1:]:
        arrived = near_part(k, state[2])
    chain = arrived
    for k in late:
        held(k, *chain)
        chain = far_part(k)
        near_part(k)
    return (projected + sum(sums)).astype(jnp.bfloat16)[None]


def solution(mesh):
    return jax.shard_map(
        shards,
        mesh=mesh,
        in_specs=(
            P("dev", "grp"),
            P("dev", "grp"),
            P("dev", "grp"),
            P(),
            P("grp", None),
            P(),
            P("dev", "grp", None),
            P("dev", "grp", None),
            P(("grp", "dev"), None, None),
            P(("grp", "dev"), None, None),
            P(("grp", "dev"), None, None),
        ),
        out_specs=P("dev", "grp", None),
        check_vma=False,
    )
```

profile of v0, /device:TPU:0, one launch (start us, length us, event | category | flops | bytes accessed | tf_op | source)
XLA Modules:
  0.0 278.0 jit_solution(9738436091211839930)
XLA Ops:
  2.4 5.2 %collective-permute-start.1 = (bf16[512,256]{1,0:T(8,128)(2,1)S(1)}, bf16[512,256]{1,0:T(8,128)(2,1)}, u32[]{:S(2)}, u32[]{:S(2)}) collective-permute-start(bf16[512,256]{1,0:T(8,128)(2,1)S(1)} %constant_dynamic-update-slice_fusion.refs_1_.refs_7_), channel_id=1, source_target_pairs={{0,2},{1,3},{2,4},{3,5},{4,6},{5,7},{8,10},{9,11},{10,12},{11,13},... | collective-permute-start | bytes 786440 | tf_op jit(solution)/shard_map/ppermute | solution.py:44
  17.1 5.2 %collective-permute-start.2 = (bf16[512,256]{1,0:T(8,128)(2,1)}, bf16[512,256]{1,0:T(8,128)(2,1)}, u32[]{:S(2)}, u32[]{:S(2)}) collective-permute-start(bf16[512,256]{1,0:T(8,128)(2,1)} %collective-permute-done.1.refs_5_), channel_id=1, source_target_pairs={{0,2},{1,3},{2,4},{3,5},{4,6},{5,7},{8,10},{9,11},{10,12},{11,13},... | collective-permute-start | bytes 786440 | tf_op jit(solution)/shard_map/ppermute | solution.py:44
  29.8 3.7 %collective-permute-start.8 = (f32[4,32,128]{2,1,0:T(8,128)S(1)}, f32[4,32,128]{2,1,0:T(8,128)}, u32[]{:S(2)}, u32[]{:S(2)}) collective-permute-start(f32[4,32,128]{2,1,0:T(8,128)S(1)} %get-tuple-element.102.refs_10_), channel_id=1, source_target_pairs={{0,6},{1,7},{2,0},{3,1},{4,2},{5,3},{6,4},{7,5},{8,14},{9,15},{10,... | collective-permute-start | bytes 196616 | tf_op jit(solution)/shard_map/ppermute | solution.py:38
  33.5 4.2 %attend.4 = bf16[128,1024]{1,0:T(8,128)(2,1)} custom-call(s32[11]{0:T(128)} %pad_add_fusion.2.bounds, bf16[512,1024]{1,0:T(8,128)(2,1)} %refs_0_.7, s32[512,1]{1,0:T(8,128)} %copy.38.refs_1_, bf16[512,256]{1,0:T(8,128)(2,1)} %collective-permute-done.refs_2_, bf16[512,256]{1,0:T(8,128)(2,1)} %collective-permute-done.2.refs_3_, ...), custom_call_target="tpu_custom_call" | custom-call | flops 939524096 | bytes 1835008 | tf_op jit(solution)/shard_map/attend/pallas_call | solution.py:157
  37.8 3.1 %convolution_convert_fusion.2.refs_9_ = bf16[128,2048]{1,0:T(8,128)(2,1)S(1)} fusion(bf16[128,1024]{1,0:T(8,128)(2,1)} %attend.4, bf16[1024,2048]{1,0:T(8,128)(2,1)} %param.15), kind=kOutput, calls=%fused_computation.5 | convolution fusion | flops 537133056 | bytes 4980736 | tf_op jit(solution)/shard_map/dot_general | solution.py:398
  43.4 4.2 %attend.6 = bf16[128,1024]{1,0:T(8,128)(2,1)} custom-call(s32[11]{0:T(128)} %pad_add_fusion.2.bounds, bf16[512,1024]{1,0:T(8,128)(2,1)} %refs_0_.7, s32[512,1]{1,0:T(8,128)} %copy.38.refs_1_, bf16[512,256]{1,0:T(8,128)(2,1)} %collective-permute-done.refs_2_, bf16[512,256]{1,0:T(8,128)(2,1)} %collective-permute-done.2.refs_3_, ...), custom_call_target="tpu_custom_call" | custom-call | flops 939524096 | bytes 1835008 | tf_op jit(solution)/shard_map/attend/pallas_call | solution.py:157
  51.2 3.0 %collective-permute-start.9 = (f32[4,32,128]{2,1,0:T(8,128)S(1)}, f32[4,32,128]{2,1,0:T(8,128)}, u32[]{:S(2)}, u32[]{:S(2)}) collective-permute-start(f32[4,32,128]{2,1,0:T(8,128)S(1)} %get-tuple-element.102.refs_10_), channel_id=1, source_target_pairs={{0,4},{1,5},{2,6},{3,7},{4,0},{5,1},{6,2},{7,3},{8,12},{9,13},{10,... | collective-permute-start | bytes 196616 | tf_op jit(solution)/shard_map/ppermute | solution.py:38
  55.1 5.4 %collective-permute-start.10 = (f32[4,32,128]{2,1,0:T(8,128)S(1)}, f32[4,32,128]{2,1,0:T(8,128)}, u32[]{:S(2)}, u32[]{:S(2)}) collective-permute-start(f32[4,32,128]{2,1,0:T(8,128)S(1)} %get-tuple-element.102.refs_10_), channel_id=1, source_target_pairs={{0,2},{1,3},{2,4},{3,5},{4,6},{5,7},{6,0},{7,1},{8,10},{9,11},{10,... | collective-permute-start | bytes 196616 | tf_op jit(solution)/shard_map/ppermute | solution.py:38
  62.6 4.4 %attend.7 = bf16[128,1024]{1,0:T(8,128)(2,1)} custom-call(s32[11]{0:T(128)} %pad_add_fusion.2.bounds, bf16[512,1024]{1,0:T(8,128)(2,1)} %refs_0_.7, s32[512,1]{1,0:T(8,128)} %copy.38.refs_1_, bf16[512,256]{1,0:T(8,128)(2,1)} %collective-permute-done.refs_2_, bf16[512,256]{1,0:T(8,128)(2,1)} %collective-permute-done.2.refs_3_, ...), custom_call_target="tpu_custom_call" | custom-call | flops 939524096 | bytes 1835008 | tf_op jit(solution)/shard_map/attend/pallas_call | solution.py:157
  74.6 4.2 %attend.5 = bf16[128,1024]{1,0:T(8,128)(2,1)} custom-call(s32[11]{0:T(128)} %pad_add_fusion.2.bounds, bf16[512,1024]{1,0:T(8,128)(2,1)} %refs_0_.7, s32[512,1]{1,0:T(8,128)} %copy.38.refs_1_, bf16[512,256]{1,0:T(8,128)(2,1)} %collective-permute-done.refs_2_, bf16[512,256]{1,0:T(8,128)(2,1)} %collective-permute-done.2.refs_3_, ...), custom_call_target="tpu_custom_call" | custom-call | flops 939524096 | bytes 1835008 | tf_op jit(solution)/shard_map/attend/pallas_call | solution.py:157
  84.9 6.5 %collective-permute-start.18 = (bf16[128,2048]{1,0:T(8,128)(2,1)S(1)}, bf16[128,2048]{1,0:T(8,128)(2,1)S(1)}, u32[]{:S(2)}, u32[]{:S(2)}) collective-permute-start(bf16[128,2048]{1,0:T(8,128)(2,1)S(1)} %multiply_convert_fusion.refs_5_), channel_id=1, source_target_pairs={{0,6},{1,7},{2,0},{3,1},{4,2},{5,3},{6,4},{7,5},{8,14},{9,15},{10,... | collective-permute-start | bytes 1572872 | tf_op jit(solution)/shard_map/ppermute | solution.py:38
  94.9 3.4 %collective-permute-start.25 = (bf16[128,2048]{1,0:T(8,128)(2,1)}, bf16[128,2048]{1,0:T(8,128)(2,1)}, u32[]{:S(2)}, u32[]{:S(2)}) collective-permute-start(bf16[128,2048]{1,0:T(8,128)(2,1)} %hold.14), channel_id=1, source_target_pairs={{0,4},{1,5},{2,6},{3,7},{4,0},{5,1},{6,2},{7,3},{8,12},{9,13},{10,... | collective-permute-start | bytes 1572872 | tf_op jit(solution)/shard_map/ppermute | solution.py:38
  98.3 4.0 %collective-permute-done.18.refs_0_ = bf16[128,2048]{1,0:T(8,128)(2,1)S(1)} collective-permute-done((bf16[128,2048]{1,0:T(8,128)(2,1)S(1)}, bf16[128,2048]{1,0:T(8,128)(2,1)S(1)}, u32[]{:S(2)}, u32[]{:S(2)}) %collective-permute-start.18) | collective-permute-done | bytes 524320 | tf_op jit(solution)/shard_map/ppermute | solution.py:38
  107.1 8.7 %collective-permute-done.26.refs_3_.refs_8_ = bf16[64,2048]{1,0:T(8,128)(2,1)S(1)} collective-permute-done((bf16[64,2048]{1,0:T(8,128)(2,1)}, bf16[64,2048]{1,0:T(8,128)(2,1)S(1)}, u32[]{:S(2)}, u32[]{:S(2)}) %collective-permute-start.26) | collective-permute-done | bytes 262176 | tf_op jit(solution)/shard_map/ppermute | solution.py:29
  115.8 3.8 %collective-permute-done.25.refs_0_ = bf16[128,2048]{1,0:T(8,128)(2,1)} collective-permute-done((bf16[128,2048]{1,0:T(8,128)(2,1)}, bf16[128,2048]{1,0:T(8,128)(2,1)}, u32[]{:S(2)}, u32[]{:S(2)}) %collective-permute-start.25) | collective-permute-done | bytes 524320 | tf_op jit(solution)/shard_map/ppermute | solution.py:38
  126.6 7.0 %collective-permute-start.32 = (bf16[128,2048]{1,0:T(8,128)(2,1)}, bf16[128,2048]{1,0:T(8,128)(2,1)}, u32[]{:S(2)}, u32[]{:S(2)}) collective-permute-start(bf16[128,2048]{1,0:T(8,128)(2,1)} %hold.16), channel_id=1, source_target_pairs={{0,2},{1,3},{2,4},{3,5},{4,6},{5,7},{6,0},{7,1},{8,10},{9,11},{10,... | collective-permute-start | bytes 1572872 | tf_op jit(solution)/shard_map/ppermute | solution.py:38
  146.8 10.9 %feed_first.2 = (bf16[384,2048]{1,0:T(8,128)(2,1)}, bf16[384,2048]{1,0:T(8,128)(2,1)}) custom-call(bf16[128,2048]{1,0:T(8,128)(2,1)} %hold.13.refs_0_, bf16[128,2048]{1,0:T(8,128)(2,1)} %copy-done.10, bf16[128,2048]{1,0:T(8,128)(2,1)} %copy-done.11, bf16[64,2048]{1,0:T(8,128)(2,1)} %copy-done.31, bf16[64,2048]{1,0:T(8,128)(2,1)} %copy-done.32, ...), custom_call_target="tpu_custom_call" | custom-call | flops 3623878656 | bytes 15728640 | tf_op jit(solution)/shard_map/feed_first/pallas_call | solution.py:302
  161.6 2.5 collective-permute-start.36
  164.2 11.9 %feed_second.2 = (bf16[128,2048]{1,0:T(8,128)(2,1)}, bf16[128,2048]{1,0:T(8,128)(2,1)}, bf16[128,2048]{1,0:T(8,128)(2,1)}, bf16[64,2048]{1,0:T(8,128)(2,1)}, bf1...) custom-call(s32[2,2,4,128]{3,2,1,0:T(4,128)} %stack.84.refs_10_.refs, ...), custom_call_target="tpu_custom_call" | custom-call | flops 3623878656 | bytes 15728640 | tf_op jit(solution)/shard_map/feed_second/pallas_call | solution.py:302
  178.8 4.7 %collective-permute-done.39.refs_15_.refs_2_ = bf16[64,2048]{1,0:T(8,128)(2,1)S(1)} collective-permute-done((bf16[64,2048]{1,0:T(8,128)(2,1)}, bf16[64,2048]{1,0:T(8,128)(2,1)S(1)}, u32[]{:S(2)}, u32[]{:S(2)}) %collective-permute-start.39) | collective-permute-done | bytes 262176 | tf_op jit(solution)/shard_map/ppermute | solution.py:25
  192.2 10.9 %feed_first.3 = (bf16[384,2048]{1,0:T(8,128)(2,1)}, bf16[384,2048]{1,0:T(8,128)(2,1)}) custom-call(bf16[128,2048]{1,0:T(8,128)(2,1)} %hold.17.refs_0_, bf16[128,2048]{1,0:T(8,128)(2,1)} %get-tuple-element.43.refs_7_.refs_1_, bf16[128,2048]{1,0:T(8,128)(2,1)} %get-tuple-element.44.refs_8_.refs_2_, bf16[64,2048]{1,0:T(8,128)(2,1)} %copy-done.27, ...), custom_call_target="tpu_custom_call" | custom-call | flops 3623878656 | bytes 15728640 | tf_op jit(solution)/shard_map/feed_first/pallas_call | solution.py:302
  208.3 2.5 add_convert_fusion.3
  210.8 12.2 %collective-permute-start.41 = (bf16[128,2048]{1,0:T(8,128)(2,1)}, bf16[128,2048]{1,0:T(8,128)(2,1)}, u32[]{:S(2)}, u32[]{:S(2)}) collective-permute-start(bf16[128,2048]{1,0:T(8,128)(2,1)} %add_convert_fusion.3), channel_id=1, source_target_pairs={{0,4},{1,5},{2,6},{3,7},{4,0},{5,1},{6,2},{7,3},{8,12},{9,13},{10,... | collective-permute-start | bytes 1572872 | tf_op jit(solution)/shard_map/ppermute | solution.py:38
  223.0 11.8 %feed_second.3 = (bf16[128,2048]{1,0:T(8,128)(2,1)}, bf16[128,2048]{1,0:T(8,128)(2,1)}, bf16[128,2048]{1,0:T(8,128)(2,1)}, bf16[64,2048]{1,0:T(8,128)(2,1)}, bf1...) custom-call(s32[2,2,4,128]{3,2,1,0:T(4,128)} %pad_add_fusion.refs_10, ...), custom_call_target="tpu_custom_call" | custom-call | flops 3623878656 | bytes 15728640 | tf_op jit(solution)/shard_map/feed_second/pallas_call | solution.py:302
  236.4 2.4 add_convert_fusion.2
  240.2 5.1 %collective-permute-done.47.refs_3_ = bf16[64,2048]{1,0:T(8,128)(2,1)S(1)} collective-permute-done((bf16[64,2048]{1,0:T(8,128)(2,1)}, bf16[64,2048]{1,0:T(8,128)(2,1)S(1)}, u32[]{:S(2)}, u32[]{:S(2)}) %collective-permute-start.47) | collective-permute-done | bytes 262176 | tf_op jit(solution)/shard_map/ppermute | solution.py:29
  251.4 4.2 %collective-permute-done.52 = bf16[64,2048]{1,0:T(8,128)(2,1)S(1)} collective-permute-done((bf16[64,2048]{1,0:T(8,128)(2,1)}, bf16[64,2048]{1,0:T(8,128)(2,1)S(1)}, u32[]{:S(2)}, u32[]{:S(2)}) %collective-permute-start.52) | collective-permute-done | bytes 262176 | tf_op jit(solution)/shard_map/ppermute | solution.py:29
  256.7 5.5 %collective-permute-done.54 = bf16[64,2048]{1,0:T(8,128)(2,1)S(1)} collective-permute-done((bf16[64,2048]{1,0:T(8,128)(2,1)}, bf16[64,2048]{1,0:T(8,128)(2,1)S(1)}, u32[]{:S(2)}, u32[]{:S(2)}) %collective-permute-start.54) | collective-permute-done | bytes 262176 | tf_op jit(solution)/shard_map/ppermute | solution.py:25
  265.7 3.3 %collective-permute-start.51 = (bf16[128,2048]{1,0:T(8,128)(2,1)S(1)}, bf16[128,2048]{1,0:T(8,128)(2,1)S(1)}, u32[]{:S(2)}, u32[]{:S(2)}) collective-permute-start(bf16[128,2048]{1,0:T(8,128)(2,1)S(1)} %add_convert_fusion.1), channel_id=1, source_target_pairs={{0,6},{1,7},{2,0},{3,1},{4,2},{5,3},{6,4},{7,5},{8,14},{9,15},{10,... | collective-permute-start | bytes 1572872 | tf_op jit(solution)/shard_map/ppermute | solution.py:38
  268.9 2.4 collective-permute-done.53
  272.6 3.1 %collective-permute-done.51 = bf16[128,2048]{1,0:T(8,128)(2,1)S(1)} collective-permute-done((bf16[128,2048]{1,0:T(8,128)(2,1)S(1)}, bf16[128,2048]{1,0:T(8,128)(2,1)S(1)}, u32[]{:S(2)}, u32[]{:S(2)}) %collective-permute-start.51) | collective-permute-done | bytes 524320 | tf_op jit(solution)/shard_map/ppermute | solution.py:38
  275.6 2.4 fusion.2
  (249 shorter events, 105.5 us)
Async XLA Ops:
  2.4 10.7 %collective-permute-start.1 = (bf16[512,256]{1,0:T(8,128)(2,1)S(1)}, bf16[512,256]{1,0:T(8,128)(2,1)}, u32[]{:S(2)}, u32[]{:S(2)}) collective-permute-start(bf16[512,256]{1,0:T(8,128)(2,1)S(1)} %constant_dynamic-update-slice_fusion.refs_1_.refs_7_), channel_id=1, source_target_pairs={{0,2},{1,3},{2,4},{3,5},{4,6},{5,7},{8,10},{9,11},{10,12},{11,13},... | collective-permute-start | bytes 786440 | tf_op jit(solution)/shard_map/ppermute | solution.py:44
  7.6 47.5 %collective-permute-start.14 = (bf16[2048,768]{1,0:T(8,128)(2,1)}, bf16[2048,768]{1,0:T(8,128)(2,1)S(1)}, u32[]{:S(2)}, u32[]{:S(2)}) collective-permute-start(bf16[2048,768]{1,0:T(8,128)(2,1)} %bitcast.39), channel_id=1, source_target_pairs={{0,1},{1,0},{2,3},{3,2},{4,5},{5,4},{6,7},{7,6},{8,9},{9,8},{10,11... | collective-permute-start | bytes 9437192 | tf_op jit(solution)/shard_map/ppermute | solution.py:33
  7.8 52.8 %collective-permute-start.15 = (bf16[2048,768]{1,0:T(8,128)(2,1)}, bf16[2048,768]{1,0:T(8,128)(2,1)}, u32[]{:S(2)}, u32[]{:S(2)}) collective-permute-start(bf16[2048,768]{1,0:T(8,128)(2,1)} %bitcast.42), channel_id=1, source_target_pairs={{0,1},{1,0},{2,3},{3,2},{4,5},{5,4},{6,7},{7,6},{8,9},{9,8},{10,11... | collective-permute-start | bytes 9437192 | tf_op jit(solution)/shard_map/ppermute | solution.py:33
  8.1 54.0 %collective-permute-start.16 = (bf16[768,2048]{1,0:T(8,128)(2,1)}, bf16[768,2048]{1,0:T(8,128)(2,1)}, u32[]{:S(2)}, u32[]{:S(2)}) collective-permute-start(bf16[768,2048]{1,0:T(8,128)(2,1)} %bitcast.45), channel_id=1, source_target_pairs={{0,1},{1,0},{2,3},{3,2},{4,5},{5,4},{6,7},{7,6},{8,9},{9,8},{10,11... | collective-permute-start | bytes 9437192 | tf_op jit(solution)/shard_map/ppermute | solution.py:33
  10.4 12.6 %collective-permute-start = (bf16[512,256]{1,0:T(8,128)(2,1)S(1)}, bf16[512,256]{1,0:T(8,128)(2,1)}, u32[]{:S(2)}, u32[]{:S(2)}) collective-permute-start(bf16[512,256]{1,0:T(8,128)(2,1)S(1)} %constant_dynamic-update-slice_fusion.refs_1_.refs_7_), channel_id=1, source_target_pairs={{1,6},{9,14},{17,22},{25,30}} | collective-permute-start | bytes 786440 | tf_op jit(solution)/shard_map/ppermute | solution.py:44
  29.8 42.5 %collective-permute-start.8 = (f32[4,32,128]{2,1,0:T(8,128)S(1)}, f32[4,32,128]{2,1,0:T(8,128)}, u32[]{:S(2)}, u32[]{:S(2)}) collective-permute-start(f32[4,32,128]{2,1,0:T(8,128)S(1)} %get-tuple-element.102.refs_10_), channel_id=1, source_target_pairs={{0,6},{1,7},{2,0},{3,1},{4,2},{5,3},{6,4},{7,5},{8,14},{9,15},{10,... | collective-permute-start | bytes 196616 | tf_op jit(solution)/shard_map/ppermute | solution.py:38
  51.2 21.1 %collective-permute-start.9 = (f32[4,32,128]{2,1,0:T(8,128)S(1)}, f32[4,32,128]{2,1,0:T(8,128)}, u32[]{:S(2)}, u32[]{:S(2)}) collective-permute-start(f32[4,32,128]{2,1,0:T(8,128)S(1)} %get-tuple-element.102.refs_10_), channel_id=1, source_target_pairs={{0,4},{1,5},{2,6},{3,7},{4,0},{5,1},{6,2},{7,3},{8,12},{9,13},{10,... | collective-permute-start | bytes 196616 | tf_op jit(solution)/shard_map/ppermute | solution.py:38
  55.1 17.2 %collective-permute-start.10 = (f32[4,32,128]{2,1,0:T(8,128)S(1)}, f32[4,32,128]{2,1,0:T(8,128)}, u32[]{:S(2)}, u32[]{:S(2)}) collective-permute-start(f32[4,32,128]{2,1,0:T(8,128)S(1)} %get-tuple-element.102.refs_10_), channel_id=1, source_target_pairs={{0,2},{1,3},{2,4},{3,5},{4,6},{5,7},{6,0},{7,1},{8,10},{9,11},{10,... | collective-permute-start | bytes 196616 | tf_op jit(solution)/shard_map/ppermute | solution.py:38
  62.1 16.8 %collective-permute-start.13 = (bf16[128,2048]{1,0:T(8,128)(2,1)}, bf16[128,2048]{1,0:T(8,128)(2,1)}, u32[]{:S(2)}, u32[]{:S(2)}) collective-permute-start(bf16[128,2048]{1,0:T(8,128)(2,1)} %pad_maximum_fusion), channel_id=1, source_target_pairs={{0,8},{8,0},{16,24},{24,16},{1,9},{9,1},{17,25},{25,17},{2,10},{10... | collective-permute-start | bytes 1572872 | tf_op jit(solution)/shard_map/ppermute | solution.py:25
  84.9 17.3 %collective-permute-start.18 = (bf16[128,2048]{1,0:T(8,128)(2,1)S(1)}, bf16[128,2048]{1,0:T(8,128)(2,1)S(1)}, u32[]{:S(2)}, u32[]{:S(2)}) collective-permute-start(bf16[128,2048]{1,0:T(8,128)(2,1)S(1)} %multiply_convert_fusion.refs_5_), channel_id=1, source_target_pairs={{0,6},{1,7},{2,0},{3,1},{4,2},{5,3},{6,4},{7,5},{8,14},{9,15},{10,... | collective-permute-start | bytes 1572872 | tf_op jit(solution)/shard_map/ppermute | solution.py:38
  94.9 24.7 %collective-permute-start.25 = (bf16[128,2048]{1,0:T(8,128)(2,1)}, bf16[128,2048]{1,0:T(8,128)(2,1)}, u32[]{:S(2)}, u32[]{:S(2)}) collective-permute-start(bf16[128,2048]{1,0:T(8,128)(2,1)} %hold.14), channel_id=1, source_target_pairs={{0,4},{1,5},{2,6},{3,7},{4,0},{5,1},{6,2},{7,3},{8,12},{9,13},{10,... | collective-permute-start | bytes 1572872 | tf_op jit(solution)/shard_map/ppermute | solution.py:38
  103.1 16.5 %collective-permute-start.21 = (bf16[128,2048]{1,0:T(8,128)(2,1)}, bf16[128,2048]{1,0:T(8,128)(2,1)S(1)}, u32[]{:S(2)}, u32[]{:S(2)}) collective-permute-start(bf16[128,2048]{1,0:T(8,128)(2,1)} %hold.13.refs_0_), channel_id=1, source_target_pairs={{0,8},{8,0},{16,24},{24,16},{1,9},{9,1},{17,25},{25,17},{2,10},{10... | collective-permute-start | bytes 1572872 | tf_op jit(solution)/shard_map/ppermute | solution.py:25
  103.1 16.6 %collective-permute-start.22 = (bf16[128,2048]{1,0:T(8,128)(2,1)}, bf16[128,2048]{1,0:T(8,128)(2,1)S(1)}, u32[]{:S(2)}, u32[]{:S(2)}) collective-permute-start(bf16[128,2048]{1,0:T(8,128)(2,1)} %hold.13.refs_0_), channel_id=1, source_target_pairs={{0,16},{8,24},{16,0},{24,8},{1,17},{9,25},{17,1},{25,9},{2,18},{10... | collective-permute-start | bytes 1572872 | tf_op jit(solution)/shard_map/ppermute | solution.py:29
  103.1 12.7 %collective-permute-start.26 = (bf16[64,2048]{1,0:T(8,128)(2,1)}, bf16[64,2048]{1,0:T(8,128)(2,1)S(1)}, u32[]{:S(2)}, u32[]{:S(2)}) collective-permute-start(bf16[64,2048]{1,0:T(8,128)(2,1)} %slice.158.refs_1_), channel_id=1, source_target_pairs={{0,16},{8,24},{16,0},{24,8},{1,17},{9,25},{17,1},{25,9},{2,18},{10... | collective-permute-start | bytes 786440 | tf_op jit(solution)/shard_map/ppermute | solution.py:29
  105.1 10.7 %collective-permute-start.27 = (bf16[64,2048]{1,0:T(8,128)(2,1)}, bf16[64,2048]{1,0:T(8,128)(2,1)S(1)}, u32[]{:S(2)}, u32[]{:S(2)}) collective-permute-start(bf16[64,2048]{1,0:T(8,128)(2,1)} %slice.159.refs_2_), channel_id=1, source_target_pairs={{0,8},{8,0},{16,24},{24,16},{1,9},{9,1},{17,25},{25,17},{2,10},{10... | collective-permute-start | bytes 786440 | tf_op jit(solution)/shard_map/ppermute | solution.py:25
  121.3 14.3 %collective-permute-start.28 = (bf16[128,2048]{1,0:T(8,128)(2,1)}, bf16[128,2048]{1,0:T(8,128)(2,1)S(1)}, u32[]{:S(2)}, u32[]{:S(2)}) collective-permute-start(bf16[128,2048]{1,0:T(8,128)(2,1)} %hold.15.refs_5_), channel_id=1, source_target_pairs={{0,8},{8,0},{16,24},{24,16},{1,9},{9,1},{17,25},{25,17},{2,10},{10... | collective-permute-start | bytes 1572872 | tf_op jit(solution)/shard_map/ppermute | solution.py:25
  121.9 15.7 %collective-permute-start.29 = (bf16[128,2048]{1,0:T(8,128)(2,1)}, bf16[128,2048]{1,0:T(8,128)(2,1)S(1)}, u32[]{:S(2)}, u32[]{:S(2)}) collective-permute-start(bf16[128,2048]{1,0:T(8,128)(2,1)} %hold.15.refs_5_), channel_id=1, source_target_pairs={{0,16},{8,24},{16,0},{24,8},{1,17},{9,25},{17,1},{25,9},{2,18},{10... | collective-permute-start | bytes 1572872 | tf_op jit(solution)/shard_map/ppermute | solution.py:29
  126.6 15.6 %collective-permute-start.32 = (bf16[128,2048]{1,0:T(8,128)(2,1)}, bf16[128,2048]{1,0:T(8,128)(2,1)}, u32[]{:S(2)}, u32[]{:S(2)}) collective-permute-start(bf16[128,2048]{1,0:T(8,128)(2,1)} %hold.16), channel_id=1, source_target_pairs={{0,2},{1,3},{2,4},{3,5},{4,6},{5,7},{6,0},{7,1},{8,10},{9,11},{10,... | collective-permute-start | bytes 1572872 | tf_op jit(solution)/shard_map/ppermute | solution.py:38
  142.8 14.9 %collective-permute-start.33 = (bf16[128,2048]{1,0:T(8,128)(2,1)}, bf16[128,2048]{1,0:T(8,128)(2,1)S(1)}, u32[]{:S(2)}, u32[]{:S(2)}) collective-permute-start(bf16[128,2048]{1,0:T(8,128)(2,1)} %hold.17.refs_0_), channel_id=1, source_target_pairs={{0,8},{8,0},{16,24},{24,16},{1,9},{9,1},{17,25},{25,17},{2,10},{10... | collective-permute-start | bytes 1572872 | tf_op jit(solution)/shard_map/ppermute | solution.py:25
  143.9 13.9 %collective-permute-start.34 = (bf16[128,2048]{1,0:T(8,128)(2,1)}, bf16[128,2048]{1,0:T(8,128)(2,1)S(1)}, u32[]{:S(2)}, u32[]{:S(2)}) collective-permute-start(bf16[128,2048]{1,0:T(8,128)(2,1)} %hold.17.refs_0_), channel_id=1, source_target_pairs={{0,16},{8,24},{16,0},{24,8},{1,17},{9,25},{17,1},{25,9},{2,18},{10... | collective-permute-start | bytes 1572872 | tf_op jit(solution)/shard_map/ppermute | solution.py:29
  159.7 16.4 %collective-permute-start.35 = (bf16[64,2048]{1,0:T(8,128)(2,1)S(1)}, bf16[64,2048]{1,0:T(8,128)(2,1)S(1)}, u32[]{:S(2)}, u32[]{:S(2)}) collective-permute-start(bf16[64,2048]{1,0:T(8,128)(2,1)S(1)} %slice.130), channel_id=1, source_target_pairs={{0,16},{8,24},{16,0},{24,8},{1,17},{9,25},{17,1},{25,9},{2,18},{10... | collective-permute-start | bytes 786440 | tf_op jit(solution)/shard_map/ppermute | solution.py:29
  161.6 14.5 %collective-permute-start.36 = (bf16[64,2048]{1,0:T(8,128)(2,1)S(1)}, bf16[64,2048]{1,0:T(8,128)(2,1)S(1)}, u32[]{:S(2)}, u32[]{:S(2)}) collective-permute-start(bf16[64,2048]{1,0:T(8,128)(2,1)S(1)} %slice.131), channel_id=1, source_target_pairs={{0,8},{8,0},{16,24},{24,16},{1,9},{9,1},{17,25},{25,17},{2,10},{10... | collective-permute-start | bytes 786440 | tf_op jit(solution)/shard_map/ppermute | solution.py:25
  185.5 22.8 %collective-permute-start.40 = (bf16[128,2048]{1,0:T(8,128)(2,1)}, bf16[128,2048]{1,0:T(8,128)(2,1)S(1)}, u32[]{:S(2)}, u32[]{:S(2)}) collective-permute-start(bf16[128,2048]{1,0:T(8,128)(2,1)} %pad_maximum_fusion.3), channel_id=1, source_target_pairs={{0,16},{8,24},{16,0},{24,8},{1,17},{9,25},{17,1},{25,9},{2,18},{10... | collective-permute-start | bytes 1572872 | tf_op jit(solution)/shard_map/ppermute | solution.py:29
  189.3 19.0 %collective-permute-start.38 = (bf16[128,2048]{1,0:T(8,128)(2,1)}, bf16[128,2048]{1,0:T(8,128)(2,1)S(1)}, u32[]{:S(2)}, u32[]{:S(2)}) collective-permute-start(bf16[128,2048]{1,0:T(8,128)(2,1)} %pad_maximum_fusion.2), channel_id=1, source_target_pairs={{0,8},{8,0},{16,24},{24,16},{1,9},{9,1},{17,25},{25,17},{2,10},{10... | collective-permute-start | bytes 1572872 | tf_op jit(solution)/shard_map/ppermute | solution.py:25
  191.6 11.6 %collective-permute-start.42 = (bf16[64,2048]{1,0:T(8,128)(2,1)}, bf16[64,2048]{1,0:T(8,128)(2,1)S(1)}, u32[]{:S(2)}, u32[]{:S(2)}) collective-permute-start(bf16[64,2048]{1,0:T(8,128)(2,1)} %get-tuple-element.59), channel_id=1, source_target_pairs={{0,16},{8,24},{16,0},{24,8},{1,17},{9,25},{17,1},{25,9},{2,18},{10... | collective-permute-start | bytes 786440 | tf_op jit(solution)/shard_map/ppermute | solution.py:29
  191.8 11.4 %collective-permute-start.44 = (bf16[64,2048]{1,0:T(8,128)(2,1)}, bf16[64,2048]{1,0:T(8,128)(2,1)S(1)}, u32[]{:S(2)}, u32[]{:S(2)}) collective-permute-start(bf16[64,2048]{1,0:T(8,128)(2,1)} %get-tuple-element.61), channel_id=1, source_target_pairs={{0,8},{8,0},{16,24},{24,16},{1,9},{9,1},{17,25},{25,17},{2,10},{10... | collective-permute-start | bytes 786440 | tf_op jit(solution)/shard_map/ppermute | solution.py:25
  204.7 30.1 %collective-permute-start.45 = (bf16[128,2048]{1,0:T(8,128)(2,1)S(1)}, bf16[128,2048]{1,0:T(8,128)(2,1)S(1)}, u32[]{:S(2)}, u32[]{:S(2)}) collective-permute-start(bf16[128,2048]{1,0:T(8,128)(2,1)S(1)} %pad_maximum_fusion.5), channel_id=1, source_target_pairs={{0,16},{8,24},{16,0},{24,8},{1,17},{9,25},{17,1},{25,9},{2,18},{10... | collective-permute-start | bytes 1572872 | tf_op jit(solution)/shard_map/ppermute | solution.py:29
  206.3 28.6 %collective-permute-start.43 = (bf16[128,2048]{1,0:T(8,128)(2,1)S(1)}, bf16[128,2048]{1,0:T(8,128)(2,1)S(1)}, u32[]{:S(2)}, u32[]{:S(2)}) collective-permute-start(bf16[128,2048]{1,0:T(8,128)(2,1)S(1)} %pad_maximum_fusion.4), channel_id=1, source_target_pairs={{0,8},{8,0},{16,24},{24,16},{1,9},{9,1},{17,25},{25,17},{2,10},{10... | collective-permute-start | bytes 1572872 | tf_op jit(solution)/shard_map/ppermute | solution.py:25
  210.8 58.1 %collective-permute-start.41 = (bf16[128,2048]{1,0:T(8,128)(2,1)}, bf16[128,2048]{1,0:T(8,128)(2,1)}, u32[]{:S(2)}, u32[]{:S(2)}) collective-permute-start(bf16[128,2048]{1,0:T(8,128)(2,1)} %add_convert_fusion.3), channel_id=1, source_target_pairs={{0,4},{1,5},{2,6},{3,7},{4,0},{5,1},{6,2},{7,3},{8,12},{9,13},{10,... | collective-permute-start | bytes 1572872 | tf_op jit(solution)/shard_map/ppermute | solution.py:38
  238.8 30.1 %collective-permute-start.46 = (bf16[128,2048]{1,0:T(8,128)(2,1)}, bf16[128,2048]{1,0:T(8,128)(2,1)S(1)}, u32[]{:S(2)}, u32[]{:S(2)}) collective-permute-start(bf16[128,2048]{1,0:T(8,128)(2,1)} %add_convert_fusion.2), channel_id=1, source_target_pairs={{0,2},{1,3},{2,4},{3,5},{4,6},{5,7},{6,0},{7,1},{8,10},{9,11},{10,... | collective-permute-start | bytes 1572872 | tf_op jit(solution)/shard_map/ppermute | solution.py:38
  247.3 16.0 %collective-permute-start.48 = (bf16[128,2048]{1,0:T(8,128)(2,1)}, bf16[128,2048]{1,0:T(8,128)(2,1)}, u32[]{:S(2)}, u32[]{:S(2)}) collective-permute-start(bf16[128,2048]{1,0:T(8,128)(2,1)} %pad_maximum_fusion.6), channel_id=1, source_target_pairs={{0,8},{8,0},{16,24},{24,16},{1,9},{9,1},{17,25},{25,17},{2,10},{10... | collective-permute-start | bytes 1572872 | tf_op jit(solution)/shard_map/ppermute | solution.py:25
  251.2 13.2 %collective-permute-start.50 = (bf16[128,2048]{1,0:T(8,128)(2,1)S(1)}, bf16[128,2048]{1,0:T(8,128)(2,1)S(1)}, u32[]{:S(2)}, u32[]{:S(2)}) collective-permute-start(bf16[128,2048]{1,0:T(8,128)(2,1)S(1)} %pad_maximum_fusion.7), channel_id=1, source_target_pairs={{0,16},{8,24},{16,0},{24,8},{1,17},{9,25},{17,1},{25,9},{2,18},{10... | collective-permute-start | bytes 1572872 | tf_op jit(solution)/shard_map/ppermute | solution.py:29
  (66 other events, 573.0 us)
where the time goes:
time: 278 us
  starting transfers between devices  97.5 us (35%)
  Pallas kernels  62.7 us (23%)
  waiting for transfers between devices  58 us (21%)
  other arithmetic  28 us (10%)
  local copies, waits for them, and re-layouts  21.9 us (8%)
  matrix products  9.31 us (3%)
    pallas_call x4, Pallas kernels, feed(): pl.pallas_call(functools.partial(feed_kernel, blocks=blocks, first=first,...  45.6 us
    ppermute x9, starting transfers between devices, turn(): lax.ppermute(value, 'dev', [(i, (i - 2 * planes) % count) for i in range(...  44.6 us
    ppermute x19, waiting for transfers between devices, swap_y(): lax.ppermute(value, 'grp', [(i, i ^ 2) for i in range(lax.axis_size('grp'...  30.1 us
    ppermute x19, starting transfers between devices, swap_x(): lax.ppermute(value, 'grp', [(i, i ^ 1) for i in range(lax.axis_size('grp'...  20.9 us
    ppermute x19, starting transfers between devices, swap_y(): lax.ppermute(value, 'grp', [(i, i ^ 2) for i in range(lax.axis_size('grp'...  18.5 us
    pallas_call x4, Pallas kernels, attend(): pl.pallas_call(functools.partial(attend_kernel, shards=len(pieces), waits...  17.1 us
    ppermute x19, waiting for transfers between devices, swap_x(): lax.ppermute(value, 'grp', [(i, i ^ 1) for i in range(lax.axis_size('grp'...  15.7 us
    ppermute x3, starting transfers between devices, earlier(): return lax.ppermute(value, 'dev', pairs)  11.7 us
  transfers between devices with their start and end apart: 56, of which 22 were waited for; matrix products, arithmetic and copies ran while one was open for 16% of the time, Pallas kernels for 23%

commit v1 on v0

--- a/solution.py
+++ b/solution.py
@@ -21,12 +21,22 @@
     return lax.optimization_barrier((value, *others))[0]
 
 
+def swap_grp(value, even, odd):
+    grp_size, dev_size = lax.axis_size("grp"), lax.axis_size("dev")
+    pairs = [
+        (g * dev_size + d, (g ^ (odd if d % 2 else even)) * dev_size + d)
+        for g in range(grp_size)
+        for d in range(dev_size)
+    ]
+    return lax.ppermute(value, ("grp", "dev"), pairs)
+
+
 def swap_x(value):
-    return lax.ppermute(value, "grp", [(i, i ^ 1) for i in range(lax.axis_size("grp"))])
+    return swap_grp(value, 1, 2)
 
 
 def swap_y(value):
-    return lax.ppermute(value, "grp", [(i, i ^ 2) for i in range(lax.axis_size("grp"))])
+    return swap_grp(value, 2, 1)
 
 
 def swap_core(value):
@@ -73,12 +83,12 @@
     return pieces
 
 
-def attend_kernel(bounds, *refs, shards, waits, mask):
+def attend_kernel(bounds, *refs, shards, waits, role):
     q_ref, start_ref = refs[:2]
     pieces = refs[2 : 2 + shards]
     out_ref, q_all, kv_ref, top, total = refs[2 + shards + waits :]
     size = pieces[0].shape[0]
-    core = bounds[2]
+    core = bounds[4]
     for i, piece in enumerate(pieces):
         lone = shards % 2
         if i < lone:
@@ -93,9 +103,9 @@
         q_all[h * rows : (h + 1) * rows, :] = q_ref[:, h * HEAD_SIZE : (h + 1) * HEAD_SIZE]
     top[...] = jnp.full_like(top, LOW)
     total[...] = jnp.zeros_like(total)
-    block_index = bounds[1] ^ mask
+    block_index = bounds[role]
     q_low = bounds[0] + block_index * rows
-    first_start, last_start = bounds[3 + 2 * block_index], bounds[4 + 2 * block_index]
+    first_start, last_start = bounds[6 + 2 * block_index], bounds[7 + 2 * block_index]
     factor = math.log2(math.e) / math.sqrt(HEAD_SIZE)
 
     def step(block, masked):
@@ -149,19 +159,19 @@
         ).astype(out_ref.dtype)
 
 
-def attend(mask, queries, pieces, starts, bounds, rows, waits=()):
+def attend(role, queries, pieces, starts, bounds, rows, waits=()):
     width = queries.shape[1]
     heads = width // HEAD_SIZE
     length = len(pieces) * pieces[0].shape[0]
     pairs = heads * rows * length // 2
     return pl.pallas_call(
-        functools.partial(attend_kernel, shards=len(pieces), waits=len(waits), mask=mask),
+        functools.partial(attend_kernel, shards=len(pieces), waits=len(waits), role=role),
         grid_spec=pltpu.PrefetchScalarGridSpec(
             num_scalar_prefetch=1,
             grid=(1,),
             in_specs=[
-                pl.BlockSpec((rows, width), lambda i, bounds: (bounds[1] ^ mask, 0)),
-                pl.BlockSpec((rows, 1), lambda i, bounds: (bounds[1] ^ mask, 0)),
+                pl.BlockSpec((rows, width), lambda i, bounds: (bounds[role], 0)),
+                pl.BlockSpec((rows, 1), lambda i, bounds: (bounds[role], 0)),
             ]
             + [pl.BlockSpec(p.shape, lambda i, bounds: (0, 0)) for p in pieces]
             + [pl.BlockSpec(memory_space=pl.ANY)] * len(waits),
@@ -387,14 +397,16 @@
     starts = jnp.sum((doc_ids[None, :] < own_docs[:, None]).astype(jnp.int32), axis=1)
     starts = starts - device * own_rows + own_low
     ends = jnp.stack([starts[::dev_rows], starts[dev_rows - 1 :: dev_rows]], axis=1)
-    bounds = jnp.concatenate([jnp.stack([own_low, group, device % 2]), ends.reshape(-1)]).astype(jnp.int32)
+    core = device % 2
+    by_role = [group ^ (1 + core), group ^ (2 - core), group ^ 3, group]
+    bounds = jnp.concatenate([jnp.stack([own_low, *by_role[:3], core, *by_role[3:]]), ends.reshape(-1)]).astype(jnp.int32)
 
     slot_of, gates, steps = routing(expert_ids[0], gate_values[0], expert_count, pieces[-2:])
     own_weights = [expert_gate[0], expert_up[0], expert_down[0]]
     other_weights = [swap_core(w) for w in own_weights]
 
-    def part(mask, *waits):
-        attended = attend(mask, queries, pieces, starts, bounds, dev_rows, waits)
+    def part(role, *waits):
+        attended = attend(role, queries, pieces, starts, bounds, dev_rows, waits)
         return jnp.dot(attended, out_weight, preferred_element_type=jnp.float32)
 
     half = dev_rows // 2
@@ -402,7 +414,7 @@
     from_a, from_b = swap_x(far[:half]), swap_y(far[half:])
     by_x = part(1, far, steps[0]).astype(jnp.bfloat16)
     by_y = part(2, by_x, steps[1], *other_weights).astype(jnp.bfloat16)
-    own = part(0, slot_of, gates, from_a, from_b)
+    own = part(5, slot_of, gates, from_a, from_b)
     projected = add_up(collect_near(own, by_x, by_y, from_a, from_b))
     normed = (
         projected

time: 278 us -> 278 us (level); the launches traced: 278 us -> 274 us
  starting transfers between devices: 97.5 us -> 84.3 us
  waiting for transfers between devices: 58 us -> 67.1 us
    ppermute x9, starting transfers between devices: 44.6 us -> 28.5 us  [turn(): lax.ppermute(value, 'dev', [(i, (i - 2 * planes) % count) for i in range(...]
    ppermute x38, waiting for transfers between devices: 45.9 us -> 58.4 us  [swap_grp(): return lax.ppermute(value, ('grp', 'dev'), pairs)]
    ppermute x9, waiting for transfers between devices: 10.9 us -> 6.12 us  [turn(): lax.ppermute(value, 'dev', [(i, (i - 2 * planes) % count) for i in range(...]
    unnamed x87 -> x89, local copies, waits for them, and re-layouts: 9.09 us -> 9.12 us
  transfers between devices with their start and end apart: 56 -> 56, of which waited for: 22 -> 21; matrix products, arithmetic and copies ran while one was open for 16% -> 17% of each run, Pallas kernels for 23% -> 23%
where the time goes in v1:
time: 278 us; the launch traced here: 274 us
  starting transfers between devices  84.3 us (30%)
  waiting for transfers between devices  67.1 us (24%)
  Pallas kernels  62.7 us (23%)
  other arithmetic  27.4 us (10%)
  local copies, waits for them, and re-layouts  22.6 us (8%)
  matrix products  9.31 us (3%)
    ppermute x38, waiting for transfers between devices, swap_grp(): return lax.ppermute(value, ('grp', 'dev'), pairs)  58.4 us
    pallas_call x4, Pallas kernels, feed(): pl.pallas_call(functools.partial(feed_kernel, blocks=blocks, first=first,...  45.6 us
    ppermute x38, starting transfers between devices, swap_grp(): return lax.ppermute(value, ('grp', 'dev'), pairs)  42 us
    ppermute x9, starting transfers between devices, turn(): lax.ppermute(value, 'dev', [(i, (i - 2 * planes) % count) for i in range(...  28.5 us
    pallas_call x4, Pallas kernels, attend(): pl.pallas_call(functools.partial(attend_kernel, shards=len(pieces), waits...  17.1 us
    ppermute x3, starting transfers between devices, earlier(): return lax.ppermute(value, 'dev', pairs)  12.2 us
    unnamed x89, local copies, waits for them, and re-layouts  9.12 us
    dot_general x4, matrix products, part(): return jnp.dot(attended, out_weight, preferred_element_type=jnp.float32)  8.57 us
  transfers between devices with their start and end apart: 56, of which 21 were waited for; matrix products, arithmetic and copies ran while one was open for 17% of the time, Pallas kernels for 23%

profile of v1, /device:TPU:0, one launch (start us, length us, event | category | flops | bytes accessed | tf_op | source)
XLA Modules:
  0.0 274.0 jit_solution(717818416927420321)
XLA Ops:
  3.0 5.6 %collective-permute-start.1 = (bf16[512,256]{1,0:T(8,128)(2,1)S(1)}, bf16[512,256]{1,0:T(8,128)(2,1)}, u32[]{:S(2)}, u32[]{:S(2)}) collective-permute-start(bf16[512,256]{1,0:T(8,128)(2,1)S(1)} %constant_dynamic-update-slice_fusion.refs_1_.refs_7_), channel_id=1, source_target_pairs={{0,2},{1,3},{2,4},{3,5},{4,6},{5,7},{8,10},{9,11},{10,12},{11,13},... | collective-permute-start | bytes 786440 | tf_op jit(solution)/shard_map/ppermute | solution.py:54
  12.1 2.5 collective-permute-done.1.refs_5_
  18.5 5.2 %collective-permute-start.2 = (bf16[512,256]{1,0:T(8,128)(2,1)}, bf16[512,256]{1,0:T(8,128)(2,1)}, u32[]{:S(2)}, u32[]{:S(2)}) collective-permute-start(bf16[512,256]{1,0:T(8,128)(2,1)} %collective-permute-done.1.refs_5_), channel_id=1, source_target_pairs={{0,2},{1,3},{2,4},{3,5},{4,6},{5,7},{8,10},{9,11},{10,12},{11,13},... | collective-permute-start | bytes 786440 | tf_op jit(solution)/shard_map/ppermute | solution.py:54
  31.6 4.8 %collective-permute-start.8 = (f32[4,32,128]{2,1,0:T(8,128)S(1)}, f32[4,32,128]{2,1,0:T(8,128)}, u32[]{:S(2)}, u32[]{:S(2)}) collective-permute-start(f32[4,32,128]{2,1,0:T(8,128)S(1)} %get-tuple-element.102.refs_10_), channel_id=1, source_target_pairs={{0,6},{1,7},{2,0},{3,1},{4,2},{5,3},{6,4},{7,5},{8,14},{9,15},{10,... | collective-permute-start | bytes 196616 | tf_op jit(solution)/shard_map/ppermute | solution.py:48
  36.4 4.2 %attend.4 = bf16[128,1024]{1,0:T(8,128)(2,1)} custom-call(s32[14]{0:T(128)} %concatenate.40.bounds, bf16[512,1024]{1,0:T(8,128)(2,1)} %refs_0_.7, s32[512,1]{1,0:T(8,128)} %copy.38.refs_1_, bf16[512,256]{1,0:T(8,128)(2,1)} %collective-permute-done.refs_2_, bf16[512,256]{1,0:T(8,128)(2,1)} %collective-permute-done.2.refs_3_, ...), custom_call_target="tpu_custom_call" | custom-call | flops 939524096 | bytes 1835008 | tf_op jit(solution)/shard_map/attend/pallas_call | solution.py:167
  40.6 3.1 %convolution_convert_fusion.2.refs_9_ = bf16[128,2048]{1,0:T(8,128)(2,1)S(1)} fusion(bf16[128,1024]{1,0:T(8,128)(2,1)} %attend.4, bf16[1024,2048]{1,0:T(8,128)(2,1)} %param.15), kind=kOutput, calls=%fused_computation.5 | convolution fusion | flops 537133056 | bytes 4980736 | tf_op jit(solution)/shard_map/dot_general | solution.py:410
  46.3 4.2 %attend.6 = bf16[128,1024]{1,0:T(8,128)(2,1)} custom-call(s32[14]{0:T(128)} %concatenate.40.bounds, bf16[512,1024]{1,0:T(8,128)(2,1)} %refs_0_.7, s32[512,1]{1,0:T(8,128)} %copy.38.refs_1_, bf16[512,256]{1,0:T(8,128)(2,1)} %collective-permute-done.refs_2_, bf16[512,256]{1,0:T(8,128)(2,1)} %collective-permute-done.2.refs_3_, ...), custom_call_target="tpu_custom_call" | custom-call | flops 939524096 | bytes 1835008 | tf_op jit(solution)/shard_map/attend/pallas_call | solution.py:167
  52.2 5.2 %collective-permute-start.9 = (f32[4,32,128]{2,1,0:T(8,128)S(1)}, f32[4,32,128]{2,1,0:T(8,128)}, u32[]{:S(2)}, u32[]{:S(2)}) collective-permute-start(f32[4,32,128]{2,1,0:T(8,128)S(1)} %get-tuple-element.102.refs_10_), channel_id=1, source_target_pairs={{0,4},{1,5},{2,6},{3,7},{4,0},{5,1},{6,2},{7,3},{8,12},{9,13},{10,... | collective-permute-start | bytes 196616 | tf_op jit(solution)/shard_map/ppermute | solution.py:48
  58.3 5.6 %collective-permute-start.10 = (f32[4,32,128]{2,1,0:T(8,128)S(1)}, f32[4,32,128]{2,1,0:T(8,128)}, u32[]{:S(2)}, u32[]{:S(2)}) collective-permute-start(f32[4,32,128]{2,1,0:T(8,128)S(1)} %get-tuple-element.102.refs_10_), channel_id=1, source_target_pairs={{0,2},{1,3},{2,4},{3,5},{4,6},{5,7},{6,0},{7,1},{8,10},{9,11},{10,... | collective-permute-start | bytes 196616 | tf_op jit(solution)/shard_map/ppermute | solution.py:48
  66.0 4.4 %attend.7 = bf16[128,1024]{1,0:T(8,128)(2,1)} custom-call(s32[14]{0:T(128)} %concatenate.40.bounds, bf16[512,1024]{1,0:T(8,128)(2,1)} %refs_0_.7, s32[512,1]{1,0:T(8,128)} %copy.38.refs_1_, bf16[512,256]{1,0:T(8,128)(2,1)} %collective-permute-done.refs_2_, bf16[512,256]{1,0:T(8,128)(2,1)} %collective-permute-done.2.refs_3_, ...), custom_call_target="tpu_custom_call" | custom-call | flops 939524096 | bytes 1835008 | tf_op jit(solution)/shard_map/attend/pallas_call | solution.py:167
  75.6 4.2 %attend.5 = bf16[128,1024]{1,0:T(8,128)(2,1)} custom-call(s32[14]{0:T(128)} %concatenate.40.bounds, bf16[512,1024]{1,0:T(8,128)(2,1)} %refs_0_.7, s32[512,1]{1,0:T(8,128)} %copy.38.refs_1_, bf16[512,256]{1,0:T(8,128)(2,1)} %collective-permute-done.refs_2_, bf16[512,256]{1,0:T(8,128)(2,1)} %collective-permute-done.2.refs_3_, ...), custom_call_target="tpu_custom_call" | custom-call | flops 939524096 | bytes 1835008 | tf_op jit(solution)/shard_map/attend/pallas_call | solution.py:167
  85.7 6.2 %collective-permute-start.18 = (bf16[128,2048]{1,0:T(8,128)(2,1)S(1)}, bf16[128,2048]{1,0:T(8,128)(2,1)S(1)}, u32[]{:S(2)}, u32[]{:S(2)}) collective-permute-start(bf16[128,2048]{1,0:T(8,128)(2,1)S(1)} %multiply_convert_fusion.refs_5_), channel_id=1, source_target_pairs={{0,6},{1,7},{2,0},{3,1},{4,2},{5,3},{6,4},{7,5},{8,14},{9,15},{10,... | collective-permute-start | bytes 1572872 | tf_op jit(solution)/shard_map/ppermute | solution.py:48
  92.7 5.5 %collective-permute-done.19.refs_1_.refs_6_ = bf16[128,2048]{1,0:T(8,128)(2,1)S(1)} collective-permute-done((bf16[128,2048]{1,0:T(8,128)(2,1)S(1)}, bf16[128,2048]{1,0:T(8,128)(2,1)S(1)}, u32[]{:S(2)}, u32[]{:S(2)}) %collective-permute-start.19) | collective-permute-done | bytes 524320 | tf_op jit(solution)/shard_map/ppermute | solution.py:31
  99.7 2.6 collective-permute-start.25
  107.2 12.9 %collective-permute-done.26.refs_3_.refs_8_ = bf16[64,2048]{1,0:T(8,128)(2,1)S(1)} collective-permute-done((bf16[64,2048]{1,0:T(8,128)(2,1)}, bf16[64,2048]{1,0:T(8,128)(2,1)S(1)}, u32[]{:S(2)}, u32[]{:S(2)}) %collective-permute-start.26) | collective-permute-done | bytes 262176 | tf_op jit(solution)/shard_map/ppermute | solution.py:31
  120.7 2.4 collective-permute-done.25.refs_0_
  133.3 5.5 %collective-permute-done.28.refs_6_.refs_1_ = bf16[128,2048]{1,0:T(8,128)(2,1)S(1)} collective-permute-done((bf16[128,2048]{1,0:T(8,128)(2,1)}, bf16[128,2048]{1,0:T(8,128)(2,1)S(1)}, u32[]{:S(2)}, u32[]{:S(2)}) %collective-permute-start.28) | collective-permute-done | bytes 524320 | tf_op jit(solution)/shard_map/ppermute | solution.py:31
  139.5 3.3 %collective-permute-start.30 = (bf16[64,2048]{1,0:T(8,128)(2,1)}, bf16[64,2048]{1,0:T(8,128)(2,1)}, u32[]{:S(2)}, u32[]{:S(2)}) collective-permute-start(bf16[64,2048]{1,0:T(8,128)(2,1)} %slice.160), channel_id=1, source_target_pairs={{0,16},{1,9},{2,18},{3,11},{4,20},{5,13},{6,22},{7,15},{8,24},{9,1... | collective-permute-start | bytes 786440 | tf_op jit(solution)/shard_map/ppermute | solution.py:31
  152.8 10.9 %feed_first.2 = (bf16[384,2048]{1,0:T(8,128)(2,1)}, bf16[384,2048]{1,0:T(8,128)(2,1)}) custom-call(bf16[128,2048]{1,0:T(8,128)(2,1)} %hold.13.refs_0_, bf16[128,2048]{1,0:T(8,128)(2,1)} %copy-done.11, bf16[128,2048]{1,0:T(8,128)(2,1)} %copy-done.12, bf16[64,2048]{1,0:T(8,128)(2,1)} %copy-done.32, bf16[64,2048]{1,0:T(8,128)(2,1)} %copy-done.33, ...), custom_call_target="tpu_custom_call" | custom-call | flops 3623878656 | bytes 15728640 | tf_op jit(solution)/shard_map/feed_first/pallas_call | solution.py:312
  169.2 11.9 %feed_second.2 = (bf16[128,2048]{1,0:T(8,128)(2,1)}, bf16[128,2048]{1,0:T(8,128)(2,1)}, bf16[128,2048]{1,0:T(8,128)(2,1)}, bf16[64,2048]{1,0:T(8,128)(2,1)}, bf1...) custom-call(s32[2,2,4,128]{3,2,1,0:T(4,128)} %stack.96.refs_10_.refs, ...), custom_call_target="tpu_custom_call" | custom-call | flops 3623878656 | bytes 15728640 | tf_op jit(solution)/shard_map/feed_second/pallas_call | solution.py:312
  184.7 4.2 %collective-permute-done.39.refs_15_.refs_2_ = bf16[64,2048]{1,0:T(8,128)(2,1)S(1)} collective-permute-done((bf16[64,2048]{1,0:T(8,128)(2,1)}, bf16[64,2048]{1,0:T(8,128)(2,1)S(1)}, u32[]{:S(2)}, u32[]{:S(2)}) %collective-permute-start.39) | collective-permute-done | bytes 262176 | tf_op jit(solution)/shard_map/ppermute | solution.py:31
  197.1 10.9 %feed_first.3 = (bf16[384,2048]{1,0:T(8,128)(2,1)}, bf16[384,2048]{1,0:T(8,128)(2,1)}) custom-call(bf16[128,2048]{1,0:T(8,128)(2,1)} %hold.17.refs_0_, bf16[128,2048]{1,0:T(8,128)(2,1)} %get-tuple-element.43.refs_7_.refs_1_, bf16[128,2048]{1,0:T(8,128)(2,1)} %get-tuple-element.44.refs_8_.refs_2_, bf16[64,2048]{1,0:T(8,128)(2,1)} %copy-done.28, ...), custom_call_target="tpu_custom_call" | custom-call | flops 3623878656 | bytes 15728640 | tf_op jit(solution)/shard_map/feed_first/pallas_call | solution.py:312
  212.9 2.5 add_convert_fusion.3
  215.4 11.8 %feed_second.3 = (bf16[128,2048]{1,0:T(8,128)(2,1)}, bf16[128,2048]{1,0:T(8,128)(2,1)}, bf16[128,2048]{1,0:T(8,128)(2,1)}, bf16[64,2048]{1,0:T(8,128)(2,1)}, bf1...) custom-call(s32[2,2,4,128]{3,2,1,0:T(4,128)} %pad_add_fusion.refs_10, ...), custom_call_target="tpu_custom_call" | custom-call | flops 3623878656 | bytes 15728640 | tf_op jit(solution)/shard_map/feed_second/pallas_call | solution.py:312
  228.7 2.4 add_convert_fusion.2
  231.1 2.2 collective-permute-start.46
  234.7 2.6 collective-permute-done.47.refs_3_
  244.0 3.3 %collective-permute-done.52 = bf16[64,2048]{1,0:T(8,128)(2,1)S(1)} collective-permute-done((bf16[64,2048]{1,0:T(8,128)(2,1)}, bf16[64,2048]{1,0:T(8,128)(2,1)S(1)}, u32[]{:S(2)}, u32[]{:S(2)}) %collective-permute-start.52) | collective-permute-done | bytes 262176 | tf_op jit(solution)/shard_map/ppermute | solution.py:31
  248.7 9.6 %collective-permute-done.54 = bf16[64,2048]{1,0:T(8,128)(2,1)S(1)} collective-permute-done((bf16[64,2048]{1,0:T(8,128)(2,1)}, bf16[64,2048]{1,0:T(8,128)(2,1)S(1)}, u32[]{:S(2)}, u32[]{:S(2)}) %collective-permute-start.54) | collective-permute-done | bytes 262176 | tf_op jit(solution)/shard_map/ppermute | solution.py:31
  263.7 5.7 %collective-permute-done.53 = bf16[128,2048]{1,0:T(8,128)(2,1)S(1)} collective-permute-done((bf16[128,2048]{1,0:T(8,128)(2,1)S(1)}, bf16[128,2048]{1,0:T(8,128)(2,1)S(1)}, u32[]{:S(2)}, u32[]{:S(2)}) %collective-permute-start.53) | collective-permute-done | bytes 524320 | tf_op jit(solution)/shard_map/ppermute | solution.py:31
  269.4 2.3 collective-permute-done.51
  271.7 2.4 fusion.2
  (251 shorter events, 103.1 us)
Async XLA Ops:
  2.4 55.9 %collective-permute-start.14 = (bf16[2048,768]{1,0:T(8,128)(2,1)}, bf16[2048,768]{1,0:T(8,128)(2,1)S(1)}, u32[]{:S(2)}, u32[]{:S(2)}) collective-permute-start(bf16[2048,768]{1,0:T(8,128)(2,1)} %bitcast.42), channel_id=1, source_target_pairs={{0,1},{1,0},{2,3},{3,2},{4,5},{5,4},{6,7},{7,6},{8,9},{9,8},{10,11... | collective-permute-start | bytes 9437192 | tf_op jit(solution)/shard_map/ppermute | solution.py:43
  2.5 61.5 %collective-permute-start.15 = (bf16[2048,768]{1,0:T(8,128)(2,1)}, bf16[2048,768]{1,0:T(8,128)(2,1)}, u32[]{:S(2)}, u32[]{:S(2)}) collective-permute-start(bf16[2048,768]{1,0:T(8,128)(2,1)} %bitcast.45), channel_id=1, source_target_pairs={{0,1},{1,0},{2,3},{3,2},{4,5},{5,4},{6,7},{7,6},{8,9},{9,8},{10,11... | collective-permute-start | bytes 9437192 | tf_op jit(solution)/shard_map/ppermute | solution.py:43
  2.9 62.0 %collective-permute-start.16 = (bf16[768,2048]{1,0:T(8,128)(2,1)}, bf16[768,2048]{1,0:T(8,128)(2,1)}, u32[]{:S(2)}, u32[]{:S(2)}) collective-permute-start(bf16[768,2048]{1,0:T(8,128)(2,1)} %bitcast.48), channel_id=1, source_target_pairs={{0,1},{1,0},{2,3},{3,2},{4,5},{5,4},{6,7},{7,6},{8,9},{9,8},{10,11... | collective-permute-start | bytes 9437192 | tf_op jit(solution)/shard_map/ppermute | solution.py:43
  9.3 15.1 %collective-permute-start = (bf16[512,256]{1,0:T(8,128)(2,1)S(1)}, bf16[512,256]{1,0:T(8,128)(2,1)}, u32[]{:S(2)}, u32[]{:S(2)}) collective-permute-start(bf16[512,256]{1,0:T(8,128)(2,1)S(1)} %constant_dynamic-update-slice_fusion.refs_1_.refs_7_), channel_id=1, source_target_pairs={{1,6},{9,14},{17,22},{25,30}} | collective-permute-start | bytes 786440 | tf_op jit(solution)/shard_map/ppermute | solution.py:54
  31.6 41.6 %collective-permute-start.8 = (f32[4,32,128]{2,1,0:T(8,128)S(1)}, f32[4,32,128]{2,1,0:T(8,128)}, u32[]{:S(2)}, u32[]{:S(2)}) collective-permute-start(f32[4,32,128]{2,1,0:T(8,128)S(1)} %get-tuple-element.102.refs_10_), channel_id=1, source_target_pairs={{0,6},{1,7},{2,0},{3,1},{4,2},{5,3},{6,4},{7,5},{8,14},{9,15},{10,... | collective-permute-start | bytes 196616 | tf_op jit(solution)/shard_map/ppermute | solution.py:48
  52.2 21.0 %collective-permute-start.9 = (f32[4,32,128]{2,1,0:T(8,128)S(1)}, f32[4,32,128]{2,1,0:T(8,128)}, u32[]{:S(2)}, u32[]{:S(2)}) collective-permute-start(f32[4,32,128]{2,1,0:T(8,128)S(1)} %get-tuple-element.102.refs_10_), channel_id=1, source_target_pairs={{0,4},{1,5},{2,6},{3,7},{4,0},{5,1},{6,2},{7,3},{8,12},{9,13},{10,... | collective-permute-start | bytes 196616 | tf_op jit(solution)/shard_map/ppermute | solution.py:48
  58.3 14.9 %collective-permute-start.10 = (f32[4,32,128]{2,1,0:T(8,128)S(1)}, f32[4,32,128]{2,1,0:T(8,128)}, u32[]{:S(2)}, u32[]{:S(2)}) collective-permute-start(f32[4,32,128]{2,1,0:T(8,128)S(1)} %get-tuple-element.102.refs_10_), channel_id=1, source_target_pairs={{0,2},{1,3},{2,4},{3,5},{4,6},{5,7},{6,0},{7,1},{8,10},{9,11},{10,... | collective-permute-start | bytes 196616 | tf_op jit(solution)/shard_map/ppermute | solution.py:48
  64.9 15.9 %collective-permute-start.13 = (bf16[128,2048]{1,0:T(8,128)(2,1)}, bf16[128,2048]{1,0:T(8,128)(2,1)}, u32[]{:S(2)}, u32[]{:S(2)}) collective-permute-start(bf16[128,2048]{1,0:T(8,128)(2,1)} %pad_maximum_fusion), channel_id=1, source_target_pairs={{0,8},{1,17},{2,10},{3,19},{4,12},{5,21},{6,14},{7,23},{8,0},{9,25... | collective-permute-start | bytes 1572872 | tf_op jit(solution)/shard_map/ppermute | solution.py:31
  84.7 13.5 %collective-permute-start.19 = (bf16[128,2048]{1,0:T(8,128)(2,1)S(1)}, bf16[128,2048]{1,0:T(8,128)(2,1)S(1)}, u32[]{:S(2)}, u32[]{:S(2)}) collective-permute-start(bf16[128,2048]{1,0:T(8,128)(2,1)S(1)} %multiply_convert_fusion.refs_5_), channel_id=1, source_target_pairs={{0,8},{1,17},{2,10},{3,19},{4,12},{5,21},{6,14},{7,23},{8,0},{9,25... | collective-permute-start | bytes 1572872 | tf_op jit(solution)/shard_map/ppermute | solution.py:31
  85.7 16.6 %collective-permute-start.18 = (bf16[128,2048]{1,0:T(8,128)(2,1)S(1)}, bf16[128,2048]{1,0:T(8,128)(2,1)S(1)}, u32[]{:S(2)}, u32[]{:S(2)}) collective-permute-start(bf16[128,2048]{1,0:T(8,128)(2,1)S(1)} %multiply_convert_fusion.refs_5_), channel_id=1, source_target_pairs={{0,6},{1,7},{2,0},{3,1},{4,2},{5,3},{6,4},{7,5},{8,14},{9,15},{10,... | collective-permute-start | bytes 1572872 | tf_op jit(solution)/shard_map/ppermute | solution.py:48
  99.7 23.5 %collective-permute-start.25 = (bf16[128,2048]{1,0:T(8,128)(2,1)}, bf16[128,2048]{1,0:T(8,128)(2,1)}, u32[]{:S(2)}, u32[]{:S(2)}) collective-permute-start(bf16[128,2048]{1,0:T(8,128)(2,1)} %hold.14), channel_id=1, source_target_pairs={{0,4},{1,5},{2,6},{3,7},{4,0},{5,1},{6,2},{7,3},{8,12},{9,13},{10,... | collective-permute-start | bytes 1572872 | tf_op jit(solution)/shard_map/ppermute | solution.py:48
  103.1 20.0 %collective-permute-start.21 = (bf16[128,2048]{1,0:T(8,128)(2,1)}, bf16[128,2048]{1,0:T(8,128)(2,1)S(1)}, u32[]{:S(2)}, u32[]{:S(2)}) collective-permute-start(bf16[128,2048]{1,0:T(8,128)(2,1)} %hold.13.refs_0_), channel_id=1, source_target_pairs={{0,8},{1,17},{2,10},{3,19},{4,12},{5,21},{6,14},{7,23},{8,0},{9,25... | collective-permute-start | bytes 1572872 | tf_op jit(solution)/shard_map/ppermute | solution.py:31
  104.6 18.5 %collective-permute-start.22 = (bf16[128,2048]{1,0:T(8,128)(2,1)}, bf16[128,2048]{1,0:T(8,128)(2,1)S(1)}, u32[]{:S(2)}, u32[]{:S(2)}) collective-permute-start(bf16[128,2048]{1,0:T(8,128)(2,1)} %hold.13.refs_0_), channel_id=1, source_target_pairs={{0,16},{1,9},{2,18},{3,11},{4,20},{5,13},{6,22},{7,15},{8,24},{9,1... | collective-permute-start | bytes 1572872 | tf_op jit(solution)/shard_map/ppermute | solution.py:31
  105.1 14.9 %collective-permute-start.26 = (bf16[64,2048]{1,0:T(8,128)(2,1)}, bf16[64,2048]{1,0:T(8,128)(2,1)S(1)}, u32[]{:S(2)}, u32[]{:S(2)}) collective-permute-start(bf16[64,2048]{1,0:T(8,128)(2,1)} %slice.158.refs_1_), channel_id=1, source_target_pairs={{0,16},{1,9},{2,18},{3,11},{4,20},{5,13},{6,22},{7,15},{8,24},{9,1... | collective-permute-start | bytes 786440 | tf_op jit(solution)/shard_map/ppermute | solution.py:31
  106.7 14.1 %collective-permute-start.27 = (bf16[64,2048]{1,0:T(8,128)(2,1)}, bf16[64,2048]{1,0:T(8,128)(2,1)S(1)}, u32[]{:S(2)}, u32[]{:S(2)}) collective-permute-start(bf16[64,2048]{1,0:T(8,128)(2,1)} %slice.159.refs_2_), channel_id=1, source_target_pairs={{0,8},{1,17},{2,10},{3,19},{4,12},{5,21},{6,14},{7,23},{8,0},{9,25... | collective-permute-start | bytes 786440 | tf_op jit(solution)/shard_map/ppermute | solution.py:31
  124.8 14.0 %collective-permute-start.28 = (bf16[128,2048]{1,0:T(8,128)(2,1)}, bf16[128,2048]{1,0:T(8,128)(2,1)S(1)}, u32[]{:S(2)}, u32[]{:S(2)}) collective-permute-start(bf16[128,2048]{1,0:T(8,128)(2,1)} %hold.15.refs_5_), channel_id=1, source_target_pairs={{0,8},{1,17},{2,10},{3,19},{4,12},{5,21},{6,14},{7,23},{8,0},{9,25... | collective-permute-start | bytes 1572872 | tf_op jit(solution)/shard_map/ppermute | solution.py:31
  126.1 16.7 %collective-permute-start.29 = (bf16[128,2048]{1,0:T(8,128)(2,1)}, bf16[128,2048]{1,0:T(8,128)(2,1)S(1)}, u32[]{:S(2)}, u32[]{:S(2)}) collective-permute-start(bf16[128,2048]{1,0:T(8,128)(2,1)} %hold.15.refs_5_), channel_id=1, source_target_pairs={{0,16},{1,9},{2,18},{3,11},{4,20},{5,13},{6,22},{7,15},{8,24},{9,1... | collective-permute-start | bytes 1572872 | tf_op jit(solution)/shard_map/ppermute | solution.py:31
  132.2 15.4 %collective-permute-start.32 = (bf16[128,2048]{1,0:T(8,128)(2,1)}, bf16[128,2048]{1,0:T(8,128)(2,1)}, u32[]{:S(2)}, u32[]{:S(2)}) collective-permute-start(bf16[128,2048]{1,0:T(8,128)(2,1)} %hold.16), channel_id=1, source_target_pairs={{0,2},{1,3},{2,4},{3,5},{4,6},{5,7},{6,0},{7,1},{8,10},{9,11},{10,... | collective-permute-start | bytes 1572872 | tf_op jit(solution)/shard_map/ppermute | solution.py:48
  132.2 14.0 %collective-permute-start.23 = (bf16[64,2048]{1,0:T(8,128)(2,1)}, bf16[64,2048]{1,0:T(8,128)(2,1)S(1)}, u32[]{:S(2)}, u32[]{:S(2)}) collective-permute-start(bf16[64,2048]{1,0:T(8,128)(2,1)} %slice.156.refs_1_), channel_id=1, source_target_pairs={{0,16},{1,9},{2,18},{3,11},{4,20},{5,13},{6,22},{7,15},{8,24},{9,1... | collective-permute-start | bytes 786440 | tf_op jit(solution)/shard_map/ppermute | solution.py:31
  132.3 13.8 %collective-permute-start.24 = (bf16[64,2048]{1,0:T(8,128)(2,1)}, bf16[64,2048]{1,0:T(8,128)(2,1)S(1)}, u32[]{:S(2)}, u32[]{:S(2)}) collective-permute-start(bf16[64,2048]{1,0:T(8,128)(2,1)} %slice.157.refs_2_), channel_id=1, source_target_pairs={{0,8},{1,17},{2,10},{3,19},{4,12},{5,21},{6,14},{7,23},{8,0},{9,25... | collective-permute-start | bytes 786440 | tf_op jit(solution)/shard_map/ppermute | solution.py:31
  147.6 16.1 %collective-permute-start.33 = (bf16[128,2048]{1,0:T(8,128)(2,1)}, bf16[128,2048]{1,0:T(8,128)(2,1)S(1)}, u32[]{:S(2)}, u32[]{:S(2)}) collective-permute-start(bf16[128,2048]{1,0:T(8,128)(2,1)} %hold.17.refs_0_), channel_id=1, source_target_pairs={{0,8},{1,17},{2,10},{3,19},{4,12},{5,21},{6,14},{7,23},{8,0},{9,25... | collective-permute-start | bytes 1572872 | tf_op jit(solution)/shard_map/ppermute | solution.py:31
  148.7 15.0 %collective-permute-start.34 = (bf16[128,2048]{1,0:T(8,128)(2,1)}, bf16[128,2048]{1,0:T(8,128)(2,1)S(1)}, u32[]{:S(2)}, u32[]{:S(2)}) collective-permute-start(bf16[128,2048]{1,0:T(8,128)(2,1)} %hold.17.refs_0_), channel_id=1, source_target_pairs={{0,16},{1,9},{2,18},{3,11},{4,20},{5,13},{6,22},{7,15},{8,24},{9,1... | collective-permute-start | bytes 1572872 | tf_op jit(solution)/shard_map/ppermute | solution.py:31
  165.7 15.5 %collective-permute-start.35 = (bf16[64,2048]{1,0:T(8,128)(2,1)S(1)}, bf16[64,2048]{1,0:T(8,128)(2,1)S(1)}, u32[]{:S(2)}, u32[]{:S(2)}) collective-permute-start(bf16[64,2048]{1,0:T(8,128)(2,1)S(1)} %slice.130), channel_id=1, source_target_pairs={{0,16},{1,9},{2,18},{3,11},{4,20},{5,13},{6,22},{7,15},{8,24},{9,1... | collective-permute-start | bytes 786440 | tf_op jit(solution)/shard_map/ppermute | solution.py:31
  191.0 21.9 %collective-permute-start.40 = (bf16[128,2048]{1,0:T(8,128)(2,1)}, bf16[128,2048]{1,0:T(8,128)(2,1)S(1)}, u32[]{:S(2)}, u32[]{:S(2)}) collective-permute-start(bf16[128,2048]{1,0:T(8,128)(2,1)} %pad_maximum_fusion.3), channel_id=1, source_target_pairs={{0,16},{1,9},{2,18},{3,11},{4,20},{5,13},{6,22},{7,15},{8,24},{9,1... | collective-permute-start | bytes 1572872 | tf_op jit(solution)/shard_map/ppermute | solution.py:31
  194.3 18.5 %collective-permute-start.38 = (bf16[128,2048]{1,0:T(8,128)(2,1)}, bf16[128,2048]{1,0:T(8,128)(2,1)S(1)}, u32[]{:S(2)}, u32[]{:S(2)}) collective-permute-start(bf16[128,2048]{1,0:T(8,128)(2,1)} %pad_maximum_fusion.2), channel_id=1, source_target_pairs={{0,8},{1,17},{2,10},{3,19},{4,12},{5,21},{6,14},{7,23},{8,0},{9,25... | collective-permute-start | bytes 1572872 | tf_op jit(solution)/shard_map/ppermute | solution.py:31
  195.4 13.3 %collective-permute-start.42 = (bf16[64,2048]{1,0:T(8,128)(2,1)}, bf16[64,2048]{1,0:T(8,128)(2,1)S(1)}, u32[]{:S(2)}, u32[]{:S(2)}) collective-permute-start(bf16[64,2048]{1,0:T(8,128)(2,1)} %get-tuple-element.59), channel_id=1, source_target_pairs={{0,16},{1,9},{2,18},{3,11},{4,20},{5,13},{6,22},{7,15},{8,24},{9,1... | collective-permute-start | bytes 786440 | tf_op jit(solution)/shard_map/ppermute | solution.py:31
  210.2 17.0 %collective-permute-start.45 = (bf16[128,2048]{1,0:T(8,128)(2,1)S(1)}, bf16[128,2048]{1,0:T(8,128)(2,1)S(1)}, u32[]{:S(2)}, u32[]{:S(2)}) collective-permute-start(bf16[128,2048]{1,0:T(8,128)(2,1)S(1)} %pad_maximum_fusion.5), channel_id=1, source_target_pairs={{0,16},{1,9},{2,18},{3,11},{4,20},{5,13},{6,22},{7,15},{8,24},{9,1... | collective-permute-start | bytes 1572872 | tf_op jit(solution)/shard_map/ppermute | solution.py:31
  211.3 15.9 %collective-permute-start.43 = (bf16[128,2048]{1,0:T(8,128)(2,1)S(1)}, bf16[128,2048]{1,0:T(8,128)(2,1)S(1)}, u32[]{:S(2)}, u32[]{:S(2)}) collective-permute-start(bf16[128,2048]{1,0:T(8,128)(2,1)S(1)} %pad_maximum_fusion.4), channel_id=1, source_target_pairs={{0,8},{1,17},{2,10},{3,19},{4,12},{5,21},{6,14},{7,23},{8,0},{9,25... | collective-permute-start | bytes 1572872 | tf_op jit(solution)/shard_map/ppermute | solution.py:31
  215.3 48.3 %collective-permute-start.41 = (bf16[128,2048]{1,0:T(8,128)(2,1)}, bf16[128,2048]{1,0:T(8,128)(2,1)}, u32[]{:S(2)}, u32[]{:S(2)}) collective-permute-start(bf16[128,2048]{1,0:T(8,128)(2,1)} %add_convert_fusion.3), channel_id=1, source_target_pairs={{0,4},{1,5},{2,6},{3,7},{4,0},{5,1},{6,2},{7,3},{8,12},{9,13},{10,... | collective-permute-start | bytes 1572872 | tf_op jit(solution)/shard_map/ppermute | solution.py:48
  231.1 32.5 %collective-permute-start.46 = (bf16[128,2048]{1,0:T(8,128)(2,1)}, bf16[128,2048]{1,0:T(8,128)(2,1)S(1)}, u32[]{:S(2)}, u32[]{:S(2)}) collective-permute-start(bf16[128,2048]{1,0:T(8,128)(2,1)} %add_convert_fusion.2), channel_id=1, source_target_pairs={{0,2},{1,3},{2,4},{3,5},{4,6},{5,7},{6,0},{7,1},{8,10},{9,11},{10,... | collective-permute-start | bytes 1572872 | tf_op jit(solution)/shard_map/ppermute | solution.py:48
  239.3 19.6 %collective-permute-start.48 = (bf16[128,2048]{1,0:T(8,128)(2,1)}, bf16[128,2048]{1,0:T(8,128)(2,1)}, u32[]{:S(2)}, u32[]{:S(2)}) collective-permute-start(bf16[128,2048]{1,0:T(8,128)(2,1)} %pad_maximum_fusion.6), channel_id=1, source_target_pairs={{0,8},{1,17},{2,10},{3,19},{4,12},{5,21},{6,14},{7,23},{8,0},{9,25... | collective-permute-start | bytes 1572872 | tf_op jit(solution)/shard_map/ppermute | solution.py:31
  243.2 17.4 %collective-permute-start.50 = (bf16[128,2048]{1,0:T(8,128)(2,1)S(1)}, bf16[128,2048]{1,0:T(8,128)(2,1)S(1)}, u32[]{:S(2)}, u32[]{:S(2)}) collective-permute-start(bf16[128,2048]{1,0:T(8,128)(2,1)S(1)} %pad_maximum_fusion.7), channel_id=1, source_target_pairs={{0,16},{1,9},{2,18},{3,11},{4,20},{5,13},{6,22},{7,15},{8,24},{9,1... | collective-permute-start | bytes 1572872 | tf_op jit(solution)/shard_map/ppermute | solution.py:31
  (67 other events, 572.1 us)
